TPU v7x, 32 devices: a whole 2x2x4 slice. The times are simulated.
32 devices in a mesh: ctx: 4 (over y, core), head: 8 (over z, x).
Axes of the slice: x: 2, y: 2, z: 4, core: 2. Of those that a mesh axis runs over, the one named last changes fastest.
Arguments:
- queries: bfloat16 [3072, 2048], P('ctx', 'head'), may hold values from -1.796875 to 1.796875
- keys: bfloat16 [3072, 2048], P('ctx', 'head'), may hold values from -1.796875 to 1.796875
- values: bfloat16 [3072, 2048], P('ctx', 'head'), may hold values from -18 to 18
- cotangent: bfloat16 [3072, 2048], P('ctx', 'head'), may hold values from -6 to 6
- decay_code: int32 [16], P('head'), may hold values from 4 to 32768, as said below
- boundaries: int32 [3072], P('ctx'), may hold values 0 or 1
Outputs:
- output: bfloat16 [3072, 2048], P('ctx', 'head')
- grad_queries: bfloat16 [3072, 2048], P('ctx', 'head')
- grad_keys: bfloat16 [3072, 2048], P('ctx', 'head')
- grad_values: bfloat16 [3072, 2048], P('ctx', 'head')
Inputs may be any that keep to these rules, and one draw needn't show every extreme that they name: Head h's decay per token is 1 - decay_code[h] * 2^-20.
All inputs are finite; a program needn't handle non-finite values. No bound on the sum of `boundaries` on one device may be relied on, other than what follows from the above.
Results may differ from a plain program's by a relative error of at most 0.0061.
Values sent between devices are 32-bit elements; how exact they have to be, the bound alone decides.
No kernel may reach another device: no remote copies, remote signals or barrier semaphores. Data moves between devices by JAX's collectives and lax.ppermute only.
A program may use at most 64 MiB of HBM per device.

v0:
```python
import math

import jax
import jax.numpy as jnp
from jax import lax
from jax.sharding import PartitionSpec as P

BLK = 256


LOG_HALF = math.log(0.5)
EPSILON = 1e-06


def prefix(part, axis, combine, identity, reverse):
    count = lax.axis_size(axis)
    place = lax.axis_index(axis)
    ahead = count - 1 - place if reverse else place
    gathered = jax.tree.map(lambda a: lax.all_gather(a, axis), part)
    state = jax.tree.map(lambda a, e: jnp.zeros_like(a) + jnp.asarray(e, a.dtype), part, identity)

    def one(hop, state):
        source = count - 1 - hop if reverse else hop
        return combine(
            state, jax.tree.map(lambda a: lax.dynamic_index_in_dim(a, source, 0, False), gathered)
        )

    return lax.fori_loop(0, ahead, one, state)


def block_decays(decay_code, boundaries, block_count):
    rates = jnp.log1p(decay_code.astype(jnp.float32) * -(2.0 ** (-20)))
    log_steps = rates[None, :] + boundaries.astype(jnp.float32)[:, None] * LOG_HALF
    return jnp.cumsum(log_steps.reshape(block_count, BLK, rates.shape[0]), axis=1)


def combine_states(earlier, subsequent):
    return (
        earlier[0] + subsequent[0],
        jnp.exp(subsequent[0])[:, None, None] * earlier[1] + subsequent[1],
    )


def shards(queries, keys, values, cotangent, decay_code, boundaries):
    token_count, local_width = queries.shape
    groups = decay_code.shape[0]
    head_size = local_width // groups
    block_count = token_count // BLK
    full_width = local_width * lax.axis_size("head")
    shape_four = (block_count, BLK, groups, head_size)
    query_blocks = queries.reshape(shape_four)
    key_blocks = keys.reshape(shape_four)
    value_blocks = values.reshape(shape_four)
    cumulative = block_decays(decay_code, boundaries, block_count)
    totals = cumulative[:, -1, :]
    inclusive = jnp.cumsum(totals, axis=0)
    exclusive = inclusive - totals
    device_total = inclusive[-1]
    causal = jnp.arange(BLK)[:, None] >= jnp.arange(BLK)[None, :]
    levels = jnp.swapaxes(cumulative, 1, 2)
    spread = levels[:, :, :, None] - levels[:, :, None, :]
    decays = jnp.exp(jnp.where(causal, spread, 0.0))
    scores = jnp.einsum(
        "bihe,bjhe->bhij", query_blocks, key_blocks, preferred_element_type=jnp.float32
    )
    weights = jnp.where(causal, scores * decays, 0.0).astype(jnp.bfloat16)
    within = jnp.einsum(
        "bhij,bjhe->bihe", weights, value_blocks, preferred_element_type=jnp.float32
    )
    beyond = jnp.exp(totals[:, None, :] - cumulative)[..., None]
    growth = jnp.exp(cumulative)[..., None]
    scaled_keys = (key_blocks * beyond).astype(jnp.bfloat16)
    key_values = jnp.einsum(
        "bjhd,bjhe->bhde", scaled_keys, value_blocks, preferred_element_type=jnp.float32
    )
    zero_state = jnp.zeros((groups, head_size, head_size), jnp.float32)
    running = zero_state
    local_prefix = []
    for which in range(block_count):
        local_prefix.append(running)
        running = jnp.exp(totals[which])[:, None, None] * running + key_values[which]
    incoming = prefix(
        (device_total, running),
        "ctx",
        combine_states,
        (jnp.zeros_like(device_total), zero_state),
        False,
    )[1]
    held_states = (
        jnp.exp(exclusive)[:, :, None, None] * incoming[None] + jnp.stack(local_prefix)
    ).astype(jnp.bfloat16)
    carried = growth * jnp.einsum(
        "bihd,bhde->bihe", query_blocks, held_states, preferred_element_type=jnp.float32
    )
    attended = (within + carried).reshape(token_count, local_width)
    squares = jnp.sum(attended * attended, axis=1)
    grad_float = cotangent.astype(jnp.float32)
    total_squares, cross = lax.psum((squares, jnp.sum(grad_float * attended, axis=1)), "head")
    scale = lax.rsqrt(total_squares / full_width + EPSILON)
    normed = attended * scale[:, None]
    slope = scale * cross
    output = normed.astype(jnp.bfloat16)
    grad_attended = (scale[:, None] * (grad_float - normed * (slope / full_width)[:, None])).astype(
        jnp.bfloat16
    )
    grad_blocks = grad_attended.reshape(shape_four)
    grad_scores = jnp.einsum(
        "bihe,bjhe->bhij", grad_blocks, value_blocks, preferred_element_type=jnp.float32
    )
    grad_weights = jnp.where(causal, grad_scores * decays, 0.0).astype(jnp.bfloat16)
    lifted = (query_blocks * growth).astype(jnp.bfloat16)
    lifted_terms = jnp.einsum(
        "bihd,bihe->bhde", lifted, grad_blocks, preferred_element_type=jnp.float32
    )
    running_grad = zero_state
    local_suffix = [zero_state] * block_count
    for which in reversed(range(block_count)):
        local_suffix[which] = running_grad
        running_grad = jnp.exp(totals[which])[:, None, None] * running_grad + lifted_terms[which]
    grad_incoming = prefix(
        (device_total, running_grad),
        "ctx",
        combine_states,
        (jnp.zeros_like(device_total), zero_state),
        True,
    )[1]
    held_grads = (
        jnp.exp(device_total[None, :] - inclusive)[:, :, None, None] * grad_incoming[None]
        + jnp.stack(local_suffix)
    ).astype(jnp.bfloat16)
    grad_queries = jnp.einsum(
        "bhij,bjhd->bihd", grad_weights, key_blocks, preferred_element_type=jnp.float32
    ) + growth * jnp.einsum(
        "bihe,bhde->bihd", grad_blocks, held_states, preferred_element_type=jnp.float32
    )
    grad_keys = jnp.einsum(
        "bhij,bihd->bjhd", grad_weights, query_blocks, preferred_element_type=jnp.float32
    ) + beyond * jnp.einsum(
        "bjhe,bhde->bjhd", value_blocks, held_grads, preferred_element_type=jnp.float32
    )
    grad_values = jnp.einsum(
        "bhij,bihe->bjhe", weights, grad_blocks, preferred_element_type=jnp.float32
    ) + beyond * jnp.einsum(
        "bjhd,bhde->bjhe", key_blocks, held_grads, preferred_element_type=jnp.float32
    )
    return (
        output,
        grad_queries.reshape(token_count, local_width).astype(jnp.bfloat16),
        grad_keys.reshape(token_count, local_width).astype(jnp.bfloat16),
        grad_values.reshape(token_count, local_width).astype(jnp.bfloat16),
    )


def solution(mesh):
    in_specs = (
        P("ctx", "head"),
        P("ctx", "head"),
        P("ctx", "head"),
        P("ctx", "head"),
        P("head"),
        P("ctx"),
    )
    out_specs = (P("ctx", "head"), P("ctx", "head"), P("ctx", "head"), P("ctx", "head"))
    return jax.shard_map(shards, mesh=mesh, in_specs=in_specs, out_specs=out_specs, check_vma=False)
```

profile of v0, /device:TPU:0, one launch (start us, length us, event | category | flops | bytes accessed | tf_op | source)
XLA Modules:
  0.0 71.4 jit_solution(11625717032093654384)
XLA Ops:
  0.6 0.7 multiply_log-plus-one_fusion
  1.4 0.7 convert_multiply_fusion.1
  2.1 1.8 %reduce-window.6 = f32[3,2,2,128]{3,2,1,0:T(2,128)S(1)} reduce-window(f32[3,2,2,128]{3,2,1,0:T(2,128)S(1)} %broadcast_add_fusion.1, f32[]{:T(128)} %constant.71.clone.1), window={size=1x1x1x128 pad=0_0x0_0x0_0x127_0}, to_apply=%region_0.0 | reduce-window | flops 195072 | bytes 12292 | tf_op jit(solution)/shard_map/reduce-window
  5.8 0.7 copy.182
  6.5 6.0 %all-gather = f32[4,1,2]{2,1,0:T(1,128)S(1)} all-gather(f32[1,1,2]{2,1,0:T(1,128)S(1)} %bitcast.107), channel_id=1, replica_groups=mesh['ctx'=4,'head'=8] {'ctx'}, dimensions={0}, use_global_device_ids=true | all-gather | bytes 40 | tf_op jit(solution)/shard_map/all_gather | solution.py:19
  12.9 1.1 %reshape.147 = bf16[3,256,2,128]{3,2,1,0:T(2,128)(2,1)S(1)} reshape(bf16[768,256]{1,0:T(8,128)(2,1)} %param.11) | data formatting | bytes 786432 | tf_op jit(solution)/shard_map/reshape | solution.py:52
  14.1 0.6 fusion.15
  14.9 7.7 %all_gather.13 = f32[4,2,128,128]{3,2,1,0:T(8,128)S(1)} all-gather(f32[1,2,128,128]{3,2,1,0:T(8,128)S(1)} %get-tuple-element.212), channel_id=1, replica_groups=mesh['ctx'=4,'head'=8] {'ctx'}, dimensions={0}, use_global_device_ids=true | all-gather | bytes 655360 | tf_op jit(solution)/shard_map/all_gather | solution.py:19
  24.2 0.6 select_convert_fusion.1
  26.1 0.6 reduce_sum.21
  28.0 21.9 %all-reduce = (f32[768]{0:T(1024)S(1)}, f32[768]{0:T(1024)S(1)}) all-reduce(f32[768]{0:T(1024)S(1)} %copy-done.18, f32[768]{0:T(1024)S(1)} %fusion.11), channel_id=1, replica_groups=mesh['ctx'=4,'head'=8] {'head'}, use_global_device_ids=true, to_apply=%region_6.7 | all-reduce | flops 1536 | bytes 12288 | tf_op jit(solution)/shard_map/psum | solution.py:98
  49.9 1.0 %fusion.13 = (bf16[768,256]{1,0:T(8,128)(2,1)S(1)}, bf16[768,256]{1,0:T(8,128)(2,1)}) fusion(bf16[768,256]{1,0:T(8,128)(2,1)S(1)} %copy-done.4, f32[96,8,2,128]{3,2,1,0:T(2,128)S(1)} %bitcast.96, f32[768]{0:T(1024)S(1)} %get-tuple-element.219, f32[768]{0:T(1024)S(1)} %get-tuple-element.220), kind=kLoop, calls=%fused_computation.30 | loop fusion | flops 1376256 | bytes 1972224 | tf_op jit(solution)/shard_map/convert_element_type | solution.py:103
  52.8 0.8 %slice_add_fusion = (f32[1,2,128,128]{3,2,1,0:T(8,128)S(1)}, f32[1,2,128,128]{3,2,1,0:T(8,128)}, f32[1,2,128,128]{3,2,1,0:T(8,128)}) fusion(f32[3,2,128,128]{3,2,1,0:T(8,128)S(1)} %fusion.16, f32[2]{0:T(128)S(1)} %copy-done.23, f32[2]{0:T(128)S(1)} %copy-done.20, f32[2]{0:T(128)S(1)} %copy-done.24), kind=kLoop, calls=%fused_computation.56 | loop fusion | flops 163840 | bytes 786456 | tf_op jit(solution)/shard_map/add | solution.py:119
  53.6 7.2 %all_gather.14 = f32[4,2,128,128]{3,2,1,0:T(8,128)S(1)} all-gather(f32[1,2,128,128]{3,2,1,0:T(8,128)S(1)} %get-tuple-element.209), channel_id=1, replica_groups=mesh['ctx'=4,'head'=8] {'ctx'}, dimensions={0}, use_global_device_ids=true | all-gather | bytes 655360 | tf_op jit(solution)/shard_map/all_gather | solution.py:19
  60.8 2.4 %while.27 = (s32[]{:T(128)}, f32[2,128,128]{2,1,0:T(8,128)S(1)}, s32[]{:T(128)}, f32[4,2]{1,0:T(4,128)}, f32[4,2,128,128]{3,2,1,0:T(8,128)S(1)}, /*index=5*/s32[]{:T(128)}, s32[]{:T(128)}, s32[]{:T(128)}, s32[]{:T(128)}) while((s32[]{:T(128)}, f32[2,128,128]{2,1,0:T(8,128)S(1)}, s32[]{:T(128)}, f32[4,2]{1,0:T(4,128)}, ...), condition=%wide.region_10.11_spmd, body=%wide.region_9.10_spmd.sunk | while | flops 65542 | bytes 393395 | solution.py:28
  60.8 0.7 exponential_bitcast_fusion.5
  61.6 0.7 exponential_bitcast_fusion.5
  62.4 0.7 exponential_bitcast_fusion.5
  63.3 0.6 select_convert_fusion
  63.9 0.9 %copy-done.2 = bf16[3,2,256,256]{3,2,1,0:T(8,128)(2,1)} copy-done((bf16[3,2,256,256]{3,2,1,0:T(8,128)(2,1)}, bf16[3,2,256,256]{3,2,1,0:T(8,128)(2,1)S(1)}, u32[]{:S(2)}) %copy-start.2) | copy-done | bytes 786456
  65.7 0.8 %copy.233 = bf16[96,8,2,128]{3,1,2,0:T(8,128)(2,1)} copy(bf16[96,8,2,128]{3,2,1,0:T(2,128)(2,1)S(1)} %bitcast.97) | data formatting | bytes 786432
  66.8 0.8 %copy-done.1 = bf16[3,2,256,256]{3,2,1,0:T(8,128)(2,1)S(1)} copy-done((bf16[3,2,256,256]{3,2,1,0:T(8,128)(2,1)S(1)}, bf16[3,2,256,256]{3,2,1,0:T(8,128)(2,1)}, u32[]{:S(2)}) %copy-start.1) | copy-done | bytes 786456
  68.4 0.8 %copy-done.3 = bf16[3,2,256,256]{3,2,1,0:T(8,128)(2,1)S(1)} copy-done((bf16[3,2,256,256]{3,2,1,0:T(8,128)(2,1)S(1)}, bf16[3,2,256,256]{3,2,1,0:T(8,128)(2,1)}, u32[]{:S(2)}) %copy-start.3) | copy-done | bytes 786456
  70.4 1.0 %copy_bitcast_fusion = (bf16[768,256]{1,0:T(8,128)(2,1)}, bf16[768,256]{1,0:T(8,128)(2,1)}) fusion(bf16[96,8,2,128]{3,2,1,0:T(2,128)(2,1)S(1)} %bitcast.99, bf16[96,8,2,128]{3,2,1,0:T(2,128)(2,1)S(1)} %bitcast.98), kind=kLoop, calls=%fused_computation.38 | loop fusion | bytes 1572864 | tf_op jit(solution)/shard_map/convert_element_type | solution.py:150
  (98 shorter events, 11.9 us)
Async XLA Ops:
  0.6 13.4 %copy-start.9 = (bf16[768,256]{1,0:T(8,128)(2,1)S(1)}, bf16[768,256]{1,0:T(8,128)(2,1)}, u32[]{:S(2)}) copy-start(bf16[768,256]{1,0:T(8,128)(2,1)} %param.12) | copy-start | bytes 1179652
  4.4 19.8 %copy-start.13 = (f32[3,2,256]{2,1,0:T(2,128)}, f32[3,2,256]{2,1,0:T(2,128)S(1)}, u32[]{:S(2)}) copy-start(f32[3,2,256]{2,1,0:T(2,128)S(1)} %reduce_window_sum.35) | copy-start | bytes 18436
  4.6 1.1 %copy-start.22 = (f32[2]{0:T(128)}, f32[2]{0:T(128)S(1)}, u32[]{:S(2)}) copy-start(f32[2]{0:T(128)S(1)} %get-tuple-element.186) | copy-start | bytes 28
  4.6 10.2 %copy-start.19 = (f32[2]{0:T(128)}, f32[2]{0:T(128)S(1)}, u32[]{:S(2)}) copy-start(f32[2]{0:T(128)S(1)} %get-tuple-element.185) | copy-start | bytes 28
  6.5 18.3 %copy-start.16 = (f32[3,2]{1,0:T(4,128)}, f32[3,2]{1,0:T(4,128)S(1)}, u32[]{:S(2)}) copy-start(f32[3,2]{1,0:T(4,128)S(1)} %copy.164) | copy-start | bytes 76
  12.9 11.3 %copy-start.11 = (pred[256,256]{1,0:T(8,128)(4,1)}, pred[256,256]{1,0:T(8,128)(4,1)S(1)}, u32[]{:S(2)}) copy-start(pred[256,256]{1,0:T(8,128)(4,1)S(1)} %iota_compare_fusion) | copy-start | bytes 196612
  14.9 10.0 %copy-start.5 = (f32[1,2,128,128]{3,2,1,0:T(8,128)}, f32[1,2,128,128]{3,2,1,0:T(8,128)S(1)}, u32[]{:S(2)}) copy-start(f32[1,2,128,128]{3,2,1,0:T(8,128)S(1)} %get-tuple-element.214) | copy-start | bytes 393220
  22.6 1.0 %copy-start.10 = (bf16[768,256]{1,0:T(8,128)(2,1)S(1)}, bf16[768,256]{1,0:T(8,128)(2,1)}, u32[]{:S(2)}) copy-start(bf16[768,256]{1,0:T(8,128)(2,1)} %param.10) | copy-start | bytes 1179652
  24.8 0.9 %copy-start = (bf16[3,2,256,256]{3,2,1,0:T(8,128)(2,1)}, bf16[3,2,256,256]{3,2,1,0:T(8,128)(2,1)S(1)}, u32[]{:S(2)}) copy-start(bf16[3,2,256,256]{3,2,1,0:T(8,128)(2,1)S(1)} %select_convert_fusion.1) | copy-start | bytes 2359300
  26.7 1.0 %copy-start.4 = (bf16[768,256]{1,0:T(8,128)(2,1)S(1)}, bf16[768,256]{1,0:T(8,128)(2,1)}, u32[]{:S(2)}) copy-start(bf16[768,256]{1,0:T(8,128)(2,1)} %param.13) | copy-start | bytes 1179652
  27.2 0.7 %copy-start.18 = (f32[768]{0:T(1024)S(1)}, f32[768]{0:T(1024)}, u32[]{:S(2)}) copy-start(f32[768]{0:T(1024)} %reduce_sum.21) | copy-start | bytes 9220
  50.9 0.9 %copy-start.6 = (f32[1,2,128,128]{3,2,1,0:T(8,128)S(1)}, f32[1,2,128,128]{3,2,1,0:T(8,128)}, u32[]{:S(2)}) copy-start(f32[1,2,128,128]{3,2,1,0:T(8,128)} %copy-done.5) | copy-start | bytes 393220
  50.9 0.9 %copy-start.17 = (f32[3,2]{1,0:T(4,128)S(1)}, f32[3,2]{1,0:T(4,128)}, u32[]{:S(2)}) copy-start(f32[3,2]{1,0:T(4,128)} %copy-done.16) | copy-start | bytes 76
  52.1 0.7 copy-start.20
  52.1 0.7 copy-start.23
  52.1 0.7 copy-start.24
  60.8 2.4 %copy-start.12 = (pred[256,256]{1,0:T(8,128)(4,1)S(1)}, pred[256,256]{1,0:T(8,128)(4,1)}, u32[]{:S(2)}) copy-start(pred[256,256]{1,0:T(8,128)(4,1)} %copy-done.11) | copy-start | bytes 196612
  60.8 2.4 %copy-start.14 = (f32[3,2,256]{2,1,0:T(2,128)S(1)}, f32[3,2,256]{2,1,0:T(2,128)}, u32[]{:S(2)}) copy-start(f32[3,2,256]{2,1,0:T(2,128)} %copy-done.13) | copy-start | bytes 18436
  63.9 0.9 %copy-start.2 = (bf16[3,2,256,256]{3,2,1,0:T(8,128)(2,1)}, bf16[3,2,256,256]{3,2,1,0:T(8,128)(2,1)S(1)}, u32[]{:S(2)}) copy-start(bf16[3,2,256,256]{3,2,1,0:T(8,128)(2,1)S(1)} %select_convert_fusion) | copy-start | bytes 2359300
  65.2 1.3 %copy-start.7 = (f32[1,2,128,128]{3,2,1,0:T(8,128)S(1)}, f32[1,2,128,128]{3,2,1,0:T(8,128)}, u32[]{:S(2)}) copy-start(f32[1,2,128,128]{3,2,1,0:T(8,128)} %get-tuple-element.210) | copy-start | bytes 393220
  65.2 1.3 %copy-start.8 = (f32[1,2,128,128]{3,2,1,0:T(8,128)S(1)}, f32[1,2,128,128]{3,2,1,0:T(8,128)}, u32[]{:S(2)}) copy-start(f32[1,2,128,128]{3,2,1,0:T(8,128)} %get-tuple-element.211) | copy-start | bytes 393220
  65.2 1.3 %copy-start.15 = (f32[3,2]{1,0:T(4,128)S(1)}, f32[3,2]{1,0:T(4,128)}, u32[]{:S(2)}) copy-start(f32[3,2]{1,0:T(4,128)} %copy.182) | copy-start | bytes 76
  66.5 1.1 %copy-start.1 = (bf16[3,2,256,256]{3,2,1,0:T(8,128)(2,1)S(1)}, bf16[3,2,256,256]{3,2,1,0:T(8,128)(2,1)}, u32[]{:S(2)}) copy-start(bf16[3,2,256,256]{3,2,1,0:T(8,128)(2,1)} %copy-done) | copy-start | bytes 2359300
  68.0 1.1 %copy-start.3 = (bf16[3,2,256,256]{3,2,1,0:T(8,128)(2,1)S(1)}, bf16[3,2,256,256]{3,2,1,0:T(8,128)(2,1)}, u32[]{:S(2)}) copy-start(bf16[3,2,256,256]{3,2,1,0:T(8,128)(2,1)} %copy-done.2) | copy-start | bytes 2359300
  (1 other events, 0.6 us)
where the time goes:
time: 71.9 us; the launch traced here: 71.4 us
  blocking collectives  42.8 us (60%)
  local copies, waits for them, and re-layouts  15.7 us (22%)
  other arithmetic  6.61 us (9%)
  matrix products  5.18 us (7%)
  between operations  1.09 us (2%)
    psum x1, blocking collectives, shards(): lax.psum((squares, jnp.sum(grad_float * attended, axis=1)), 'head')  21.9 us
    all_gather x3, blocking collectives, prefix(): gathered = jax.tree.map(lambda a: lax.all_gather(a, axis), part)  20.9 us
    unnamed x51, local copies, waits for them, and re-layouts  6.01 us
    exp x3, local copies, waits for them, and re-layouts, combine_states(): jnp.exp(subsequent[0])[:, None, None] * earlier[1] + subsequent[1]  2.06 us
    another operation x3, other arithmetic  1.92 us

commit v1 on v0

v1 whole, which is shorter than its diff:
```python
import functools
import math

import jax
import jax.numpy as jnp
from jax import lax
from jax.experimental import pallas as pl
from jax.experimental.pallas import tpu as pltpu
from jax.sharding import PartitionSpec as P

BLK = 256
LANES = 128
LOG_TWO = math.log(2.0)
EPSILON = 1e-06
F32 = jnp.float32
BF16 = jnp.bfloat16

NN = (((1,), (0,)), ((), ()))
NT = (((1,), (1,)), ((), ()))
TN = (((0,), (0,)), ((), ()))


def mm(a, b, dims=NN):
    return lax.dot_general(a, b, dims, preferred_element_type=F32)


def iota(shape, axis):
    return lax.broadcasted_iota(jnp.int32, shape, axis)


def up8(n):
    return -(-n // 8) * 8


def halves(x):
    head = x.astype(BF16)
    return head, (x - head.astype(F32)).astype(BF16)


class Steps:
    def __init__(self, bnd_ref, code_ref, blocks, heads):
        self.blocks, self.heads, self.size = blocks, heads, blocks * heads
        rows = up8(self.size)
        per = BLK // LANES
        bnd = bnd_ref[...].astype(F32)
        parts = []
        for b in range(blocks):
            row = jnp.concatenate([bnd[b * per + i : b * per + i + 1] for i in range(per)], axis=1)
            parts += [row] * heads
        if rows > self.size:
            parts.append(jnp.zeros((rows - self.size, BLK), F32))
        marks = jnp.concatenate(parts, axis=0).astype(BF16)
        upper = (iota((BLK, BLK), 0) <= iota((BLK, BLK), 1)).astype(F32).astype(BF16)
        self.count = mm(marks, upper)
        count_all = mm(marks, jnp.ones((BLK, BLK), BF16))
        which = iota((rows, BLK), 0)
        code = jnp.zeros((rows, BLK), F32)
        for h in range(heads):
            code = jnp.where(which % heads == h, code_ref[h].astype(F32), code)
        self.rate = jnp.log1p(code * -(2.0 ** (-20)))
        place = (iota((rows, BLK), 1) + 1).astype(F32)
        self.level = self.rate * place - LOG_TWO * self.count
        self.total = self.rate * float(BLK) - LOG_TWO * count_all
        self.growth = jnp.exp(self.level)
        self.beyond = jnp.exp(self.total - self.level)
        self.decay = jnp.exp(self.total)

    def row(self, a, b, h):
        r = b * self.heads + h
        return a[r : r + 1]

    def device_total(self, h):
        return sum(self.row(self.total, b, h) for b in range(self.blocks))[:, :LANES]

    def columns(self, a, head_size):
        head, rest = halves(a)
        both = jnp.concatenate([head.astype(F32), rest.astype(F32)], axis=0).astype(BF16)
        rows, width = a.shape[0], self.heads * head_size
        result = []
        for b in range(self.blocks):
            wanted = b * self.heads + iota((2 * rows, width), 1) // head_size
            pick = (iota((2 * rows, width), 0) % rows == wanted).astype(F32).astype(BF16)
            result.append(mm(both, pick, TN))
        return result

    def decays(self, b):
        rows = self.count.shape[0]
        pick = (iota((rows, BLK), 0) == b * self.heads).astype(F32).astype(BF16)
        count_i = mm(self.count.astype(BF16), pick, TN)
        halved = LOG_TWO * (count_i - self.row(self.count, b, 0))
        apart = iota((BLK, BLK), 0) - iota((BLK, BLK), 1)
        causal = apart >= 0
        steps = apart.astype(F32)
        return causal, [
            jnp.exp(jnp.where(causal, self.row(self.rate, b, h) * steps - halved, 0.0))
            for h in range(self.heads)
        ]


def incoming(payloads, place, masks, h, head_size, heads, reverse):
    at = heads * head_size + h
    totals = [p[at : at + 1, :] for p in payloads]
    sources = [place ^ m for m in masks]

    def before(a, b):
        return a > b if reverse else a < b

    result = jnp.zeros((head_size, head_size), F32)
    for i, m in enumerate(masks):
        if m == 0:
            continue
        inner = jnp.zeros_like(totals[0])
        for j, other in enumerate(masks):
            if other in (0, m):
                continue
            between = jnp.logical_and(before(sources[i], sources[j]), before(sources[j], place))
            inner = inner + jnp.where(between, totals[j], 0.0)
        weight = jnp.where(before(sources[i], place), jnp.exp(inner), 0.0)
        result = result + weight * payloads[i][h * head_size : (h + 1) * head_size, :]
    return result


def store_totals(payload_ref, st, head_size):
    rest = [st.device_total(h) for h in range(st.heads)]
    pad = up8(st.heads) - st.heads
    if pad:
        rest.append(jnp.zeros((pad, LANES), F32))
    payload_ref[st.heads * head_size :, :] = jnp.concatenate(rest, axis=0)


def sizes(x_ref, code_ref):
    tokens, width = x_ref.shape
    heads = code_ref.shape[0]
    return tokens // BLK, heads, width // heads


def block(ref, b, h, e):
    return ref[b * BLK : (b + 1) * BLK, h * e : (h + 1) * e]


def states_kernel(code_ref, bnd_ref, k_ref, v_ref, payload_ref, local_ref):
    nb, heads, e = sizes(k_ref, code_ref)
    st = Steps(bnd_ref, code_ref, nb, heads)
    for h in range(heads):
        running = None
        for b in range(nb):
            scaled = (block(k_ref, b, h, e).T.astype(F32) * st.row(st.beyond, b, h)).astype(BF16)
            term = mm(scaled, block(v_ref, b, h, e))
            running = term if running is None else st.row(st.decay, b, h)[:, :e] * running + term
            if b < nb - 1:
                local_ref[b, h] = running
        payload_ref[h * e : (h + 1) * e, :] = running
    store_totals(payload_ref, st, e)


def within_kernel(code_ref, bnd_ref, q_ref, k_ref, v_ref, w_ref, within_ref):
    nb, heads, e = sizes(k_ref, code_ref)
    st = Steps(bnd_ref, code_ref, nb, heads)
    for b in range(nb):
        causal, decays = st.decays(b)
        for h in range(heads):
            scores = mm(block(q_ref, b, h, e), block(k_ref, b, h, e), NT)
            weights = jnp.where(causal, scores * decays[h], 0.0).astype(BF16)
            w_ref[b, h] = weights
            within_ref[b * BLK : (b + 1) * BLK, h * e : (h + 1) * e] = mm(
                weights, block(v_ref, b, h, e)
            )


def attend_kernel(masks, code_ref, place_ref, bnd_ref, q_ref, cot_ref, within_ref, local_ref, *refs):
    payloads, (held_ref, att_ref, sums_ref) = refs[: len(masks)], refs[len(masks) :]
    nb, heads, e = sizes(q_ref, code_ref)
    st = Steps(bnd_ref, code_ref, nb, heads)
    growth = st.columns(st.growth, e)
    for h in range(heads):
        arrived = incoming(payloads, place_ref[0], masks, h, e, heads, False)
        ahead = jnp.zeros((1, BLK), F32)
        for b in range(nb):
            state = jnp.exp(ahead)[:, :e] * arrived
            if b:
                state = state + local_ref[b - 1, h]
            ahead = ahead + st.row(st.total, b, h)
            held_ref[b, h] = state.astype(BF16)
    ones = jnp.ones((8, heads * e), BF16)
    squares, crosses = [], []
    for b in range(nb):
        rows = slice(b * BLK, (b + 1) * BLK)
        carried = jnp.concatenate(
            [mm(block(q_ref, b, h, e), held_ref[b, h]) for h in range(heads)], axis=1
        )
        att = within_ref[rows, :] + growth[b] * carried
        att_ref[rows, :] = att
        for dest, term in ((squares, att * att), (crosses, att * cot_ref[rows, :].astype(F32))):
            dest.append(sum(mm(ones, part, NT) for part in halves(term))[:1])
    parts = squares + crosses
    if up8(2 * nb) > 2 * nb:
        parts.append(jnp.zeros((up8(2 * nb) - 2 * nb, BLK), F32))
    sums_ref[...] = jnp.concatenate(parts, axis=0)


def norm_factors(sums, st, full_width):
    nb = st.blocks
    squares, crosses = sums[:nb], sums[nb : 2 * nb]
    scale = lax.rsqrt(squares / full_width + EPSILON)
    lean = scale * scale * crosses / full_width
    return scale, lean


def spread(rows_of, width):
    count = rows_of[0].shape[0]
    stacked = jnp.concatenate(rows_of, axis=0)
    have = stacked.shape[0]
    if up8(have) > have:
        stacked = jnp.concatenate([stacked, jnp.zeros((up8(have) - have, BLK), F32)], axis=0)
    rows = stacked.shape[0]
    head, rest = halves(stacked)
    both = jnp.concatenate([head.astype(F32), rest.astype(F32)], axis=0).astype(BF16)
    result = []
    for r in range(have):
        pick = (iota((2 * rows, width), 0) % rows == r).astype(F32).astype(BF16)
        result.append(mm(both, pick, TN))
    return [result[i * count : (i + 1) * count] for i in range(len(rows_of))]


def grad_kernel(full_width, parts, code_ref, bnd_ref, q_ref, cot_ref, att_ref, *refs):
    sums_refs, (g_ref, total_ref, payload_ref, local_ref) = refs[:parts], refs[parts:]
    nb, heads, e = sizes(q_ref, code_ref)
    st = Steps(bnd_ref, code_ref, nb, heads)
    sums = sum(ref[...] for ref in sums_refs)
    total_ref[...] = sums
    scale, lean = spread(norm_factors(sums, st, full_width), heads * e)
    for b in range(nb):
        rows = slice(b * BLK, (b + 1) * BLK)
        g_ref[rows, :] = (
            scale[b] * (cot_ref[rows, :].astype(F32) - att_ref[rows, :] * lean[b])
        ).astype(BF16)
    for h in range(heads):
        running = None
        for b in reversed(range(nb)):
            lifted = (block(q_ref, b, h, e).T.astype(F32) * st.row(st.growth, b, h)).astype(BF16)
            term = mm(lifted, block(g_ref, b, h, e))
            running = term if running is None else st.row(st.decay, b, h)[:, :e] * running + term
            if b:
                local_ref[b - 1, h] = running
        payload_ref[h * e : (h + 1) * e, :] = running
    store_totals(payload_ref, st, e)


def inner_grads_kernel(
    full_width, code_ref, bnd_ref, q_ref, k_ref, v_ref, g_ref, w_ref, held_ref, att_ref, total_ref,
    out_ref, gq_ref, gk_ref, gv_ref,
):
    nb, heads, e = sizes(q_ref, code_ref)
    st = Steps(bnd_ref, code_ref, nb, heads)
    scale = lax.rsqrt(total_ref[:nb, :] / full_width + EPSILON)
    (scale,) = spread((scale,), heads * e)
    growth = st.columns(st.growth, e)
    for b in range(nb):
        rows = slice(b * BLK, (b + 1) * BLK)
        out_ref[rows, :] = (att_ref[rows, :] * scale[b]).astype(BF16)
        causal, decays = st.decays(b)
        for h in range(heads):
            cols = slice(h * e, (h + 1) * e)
            g = block(g_ref, b, h, e)
            scores = mm(g, block(v_ref, b, h, e), NT)
            gw = jnp.where(causal, scores * decays[h], 0.0).astype(BF16)
            gq = mm(gw, block(k_ref, b, h, e)) + growth[b][:, cols] * mm(g, held_ref[b, h], NT)
            gq_ref[rows, cols] = gq.astype(BF16)
            gk_ref[rows, cols] = mm(gw, block(q_ref, b, h, e), TN)
            gv_ref[rows, cols] = mm(w_ref[b, h], g, TN)


def outer_grads_kernel(
    masks, code_ref, place_ref, bnd_ref, k_ref, v_ref, gk_part_ref, gv_part_ref, local_ref, *refs
):
    payloads, (gk_ref, gv_ref) = refs[: len(masks)], refs[len(masks) :]
    nb, heads, e = sizes(k_ref, code_ref)
    st = Steps(bnd_ref, code_ref, nb, heads)
    beyond = st.columns(st.beyond, e)
    for h in range(heads):
        cols = slice(h * e, (h + 1) * e)
        arrived = incoming(payloads, place_ref[0], masks, h, e, heads, True)
        behind = jnp.zeros((1, BLK), F32)
        for b in reversed(range(nb)):
            rows = slice(b * BLK, (b + 1) * BLK)
            state = jnp.exp(behind)[:, :e] * arrived
            if b < nb - 1:
                state = state + local_ref[b, h]
            behind = behind + st.row(st.total, b, h)
            held = state.astype(BF16)
            far = beyond[b][:, cols]
            gk = gk_part_ref[rows, cols] + far * mm(block(v_ref, b, h, e), held, NT)
            gk_ref[rows, cols] = gk.astype(BF16)
            gv = gv_part_ref[rows, cols] + far * mm(block(k_ref, b, h, e), held)
            gv_ref[rows, cols] = gv.astype(BF16)


def call(kernel, name, args, outs, flops):
    smem = [a.ndim == 1 for a in args]
    traffic = sum(a.size * a.dtype.itemsize for a in args) + sum(
        math.prod(s) * jnp.dtype(d).itemsize for s, d in outs
    )
    return pl.pallas_call(
        kernel,
        out_shape=[jax.ShapeDtypeStruct(s, d) for s, d in outs],
        in_specs=[
            pl.BlockSpec(memory_space=pltpu.SMEM if s else pltpu.VMEM) for s in smem
        ],
        out_specs=[pl.BlockSpec(memory_space=pltpu.VMEM) for _ in outs],
        compiler_params=pltpu.CompilerParams(vmem_limit_bytes=40 * 2**20),
        cost_estimate=pl.CostEstimate(flops=flops, bytes_accessed=traffic, transcendentals=0),
        name=name,
    )(*args)


def swap(a, axis, mask):
    return lax.ppermute(a, axis, [(i, i ^ mask) for i in range(lax.axis_size(axis))])


def gather_states(payload):
    masks, held = [0], [payload]
    bit = lax.axis_size("ctx") // 2
    while bit:
        held += [swap(a, "ctx", bit) for a in held]
        masks += [m | bit for m in masks]
        bit //= 2
    return masks, held


def sum_over_heads(sums):
    size = lax.axis_size("head")
    parts, bit, width = [sums], 1, 2
    while bit < size:
        own = functools.reduce(jnp.add, parts)
        width = min(width, size // bit)
        parts = [own] + [swap(own, "head", bit * i) for i in range(1, width)]
        bit, width = bit * width, 4
    return parts


def shards(queries, keys, values, cotangent, decay_code, boundaries):
    tokens, width = queries.shape
    heads = decay_code.shape[0]
    e = width // heads
    nb = tokens // BLK
    full_width = width * lax.axis_size("head")
    bnd = boundaries.reshape(tokens // LANES, LANES)
    place = lax.axis_index("ctx").astype(jnp.int32).reshape(1)
    payload = ((heads * e + up8(heads), LANES), F32)
    local = ((max(nb - 1, 1), heads, e, e), F32)
    big = 2 * tokens * heads * e * BLK
    small = 2 * tokens * heads * e * e

    state, prefix = call(
        states_kernel, "states", (decay_code, bnd, keys, values), (payload, local), small
    )
    masks, states = gather_states(state)
    weights, within = call(
        within_kernel, "within", (decay_code, bnd, queries, keys, values),
        (((nb, heads, BLK, BLK), BF16), ((tokens, width), F32)), 2 * big,
    )
    held, attended, sums = call(
        functools.partial(attend_kernel, masks), "attend",
        (decay_code, place, bnd, queries, cotangent, within, prefix, *states),
        (((nb, heads, e, e), BF16), ((tokens, width), F32), ((up8(2 * nb), BLK), F32)), small,
    )
    sums = sum_over_heads(sums)
    grad, totals, grad_state, suffix = call(
        functools.partial(grad_kernel, full_width, len(sums)), "grad",
        (decay_code, bnd, queries, cotangent, attended, *sums),
        (((tokens, width), BF16), ((up8(2 * nb), BLK), F32), payload, local), small,
    )
    masks, grad_states = gather_states(grad_state)
    output, grad_queries, gk_part, gv_part = call(
        functools.partial(inner_grads_kernel, full_width), "inner_grads",
        (decay_code, bnd, queries, keys, values, grad, weights, held, attended, totals),
        (((tokens, width), BF16), ((tokens, width), BF16), ((tokens, width), F32), ((tokens, width), F32)),
        4 * big + small,
    )
    grad_keys, grad_values = call(
        functools.partial(outer_grads_kernel, masks), "outer_grads",
        (decay_code, place, bnd, keys, values, gk_part, gv_part, suffix, *grad_states),
        (((tokens, width), BF16), ((tokens, width), BF16)), 2 * small,
    )
    return output, grad_queries, grad_keys, grad_values


def solution(mesh):
    both = P("ctx", "head")
    return jax.shard_map(
        shards,
        mesh=mesh,
        in_specs=(both, both, both, both, P("head"), P("ctx")),
        out_specs=(both, both, both, both),
        check_vma=False,
    )
```

time: 71.9 us -> 42.2 us (0.59)
  blocking collectives: 42.8 us -> 0 us
  waiting for transfers between devices: 0 us -> 14.5 us
  Pallas kernels: 0 us -> 11.6 us
  local copies, waits for them, and re-layouts: 15.7 us -> 4.33 us
  starting transfers between devices: 0 us -> 10.7 us
  other arithmetic: 6.61 us -> 0.01 us
  matrix products: 5.18 us -> 0 us
    psum x1 -> x0, blocking collectives: 21.9 us -> none  [shards(): lax.psum((squares, jnp.sum(grad_float * attended, axis=1)), 'head')]
    all_gather x3 -> x0, blocking collectives: 20.9 us -> none  [prefix(): gathered = jax.tree.map(lambda a: lax.all_gather(a, axis), part)]
    ppermute x0 -> x10, waiting for transfers between devices: none -> 14.5 us  [swap(): lax.ppermute(a, axis, [(i, i ^ mask) for i in range(lax.axis_size(axis))])]
    pallas_call x0 -> x6, Pallas kernels: none -> 11.6 us  [call(): pl.pallas_call(kernel, out_shape=[jax.ShapeDtypeStruct(s, d) for s, d in...]
    ppermute x0 -> x10, starting transfers between devices: none -> 10.7 us  [swap(): lax.ppermute(a, axis, [(i, i ^ mask) for i in range(lax.axis_size(axis))])]
    dot_general x12 -> x0, matrix products: 5.18 us -> none  [the longest x1 0.63 us: shards(): jnp.einsum('bjhd,bjhe->bhde', scaled_keys, value_blocks, preferred_elemen...]
    exp x6 -> x0, local copies, waits for them, and re-layouts: 3.05 us -> none  [the longest x3 2.06 us: combine_states(): jnp.exp(subsequent[0])[:, None, None] * earlier[1] + subsequent[1]]
    reshape x6 -> x0, local copies, waits for them, and re-layouts: 2.25 us -> none  [the longest x1 1.12 us: shards(): key_blocks = keys.reshape(shape_four)]
  transfers between devices with their start and end apart: 0 -> 10, of which waited for: 0 -> 5; matrix products, arithmetic and copies ran while one was open for 0% -> 0% of each run, Pallas kernels for 0% -> 13%
where the time goes in v1:
time: 42.2 us; the launch traced here: 41.8 us
  waiting for transfers between devices  14.5 us (34%)
  Pallas kernels  11.6 us (27%)
  starting transfers between devices  10.7 us (25%)
  local copies, waits for them, and re-layouts  4.33 us (10%)
  between operations  0.73 us (2%)
    ppermute x10, waiting for transfers between devices, swap(): lax.ppermute(a, axis, [(i, i ^ mask) for i in range(lax.axis_size(axis))])  14.5 us
    pallas_call x6, Pallas kernels, call(): pl.pallas_call(kernel, out_shape=[jax.ShapeDtypeStruct(s, d) for s, d in...  11.6 us
    ppermute x10, starting transfers between devices, swap(): lax.ppermute(a, axis, [(i, i ^ mask) for i in range(lax.axis_size(axis))])  10.7 us
    unnamed x18, local copies, waits for them, and re-layouts  4.33 us
  transfers between devices with their start and end apart: 10, of which 5 were waited for; matrix products, arithmetic and copies ran while one was open for 0% of the time, Pallas kernels for 13%

profile of v1, /device:TPU:0, one launch (start us, length us, event | category | flops | bytes accessed | tf_op | source)
XLA Modules:
  0.0 41.8 jit_solution(2602098086967560886)
XLA Ops:
  0.6 0.6 %copy-done.8 = s32[2]{0:T(128)S(1)} copy-done((s32[2]{0:T(128)S(1)}, s32[2]{0:T(128)}, u32[]{:S(2)}) %copy-start.8) | copy-done | bytes 32
  1.3 1.0 %copy-done.1 = bf16[768,256]{1,0:T(8,128)(2,1)S(1)} copy-done((bf16[768,256]{1,0:T(8,128)(2,1)S(1)}, bf16[768,256]{1,0:T(8,128)(2,1)}, u32[]{:S(2)}) %copy-start.1) | copy-done | bytes 393240
  2.3 1.0 %copy-done.3 = bf16[768,256]{1,0:T(8,128)(2,1)S(1)} copy-done((bf16[768,256]{1,0:T(8,128)(2,1)S(1)}, bf16[768,256]{1,0:T(8,128)(2,1)}, u32[]{:S(2)}) %copy-start.3) | copy-done | bytes 393240
  3.3 0.7 %copy-done.6 = s32[768]{0:T(1024)S(1)} copy-done((s32[768]{0:T(1024)S(1)}, s32[768]{0:T(1024)}, u32[]{:S(2)}) %copy-start.6) | copy-done | bytes 3096
  4.0 0.9 %states.1 = (f32[264,128]{1,0:T(8,128)S(1)}, f32[2,2,128,128]{3,2,1,0:T(8,128)S(1)}) custom-call(s32[2]{0:T(128)S(1)} %copy-done.8, s32[6,128]{1,0:T(8,128)S(1)} %bitcast.2, bf16[768,256]{1,0:T(8,128)(2,1)S(1)} %copy-done.1, bf16[768,256]{1,0:T(8,128)(2,1)S(1)} %copy-done.3), custom_call_target="tpu_custom_call" | custom-call | flops 50331648 | bytes 1186824 | tf_op jit(solution)/shard_map/states/pallas_call | solution.py:303
  4.9 0.0 copy-start.7
  4.9 3.0 %collective-permute-start = (f32[264,128]{1,0:T(8,128)S(1)}, f32[264,128]{1,0:T(8,128)S(1)}, u32[]{:S(2)}, u32[]{:S(2)}) collective-permute-start(f32[264,128]{1,0:T(8,128)S(1)} %get-tuple-element.23.refs_0_), channel_id=1, source_target_pairs={{0,16},{8,24},{16,0},{24,8},{1,17},{9,25},{17,1},{25,9},{2,18},{10... | collective-permute-start | bytes 405512 | tf_op jit(solution)/shard_map/ppermute | solution.py:317
  8.0 3.6 %collective-permute-done.refs_1_ = f32[264,128]{1,0:T(8,128)S(1)} collective-permute-done((f32[264,128]{1,0:T(8,128)S(1)}, f32[264,128]{1,0:T(8,128)S(1)}, u32[]{:S(2)}, u32[]{:S(2)}) %collective-permute-start) | collective-permute-done | bytes 135200 | tf_op jit(solution)/shard_map/ppermute | solution.py:317
  11.6 0.0 copy-start.4
  11.6 1.0 %copy-done.4 = bf16[768,256]{1,0:T(8,128)(2,1)S(1)} copy-done((bf16[768,256]{1,0:T(8,128)(2,1)S(1)}, bf16[768,256]{1,0:T(8,128)(2,1)}, u32[]{:S(2)}) %copy-start.4) | copy-done | bytes 393240
  12.6 1.7 %within.1 = (bf16[3,2,256,256]{3,2,1,0:T(8,128)(2,1)S(1)}, f32[768,256]{1,0:T(8,128)S(1)}) custom-call(s32[2]{0:T(128)S(1)} %copy-done.8, s32[6,128]{1,0:T(8,128)S(1)} %bitcast.3, bf16[768,256]{1,0:T(8,128)(2,1)S(1)} %copy-done, bf16[768,256]{1,0:T(8,128)(2,1)S(1)} %copy-done.2, bf16[768,256]{1,0:T(8,128)(2,1)S(1)} %copy-done.4), custom_call_target="tpu_custom_call" | custom-call | flops 201326592 | bytes 2755592 | tf_op jit(solution)/shard_map/within/pallas_call | solution.py:303
  14.3 2.0 %attend.1 = (bf16[3,2,128,128]{3,2,1,0:T(8,128)(2,1)S(1)}, f32[768,256]{1,0:T(8,128)S(1)}, f32[8,256]{1,0:T(8,128)S(1)}) custom-call(s32[2]{0:T(128)S(1)} %copy-done.8, s32[1]{0:T(128)} %bitcast.1.place_ref, s32[6,128]{1,0:T(8,128)S(1)} %bitcast.4, bf16[768,256]{1,0:T(8,128)(2,1)S(1)} %copy-done, bf16[768,256]{1,0:T(8,128)(2,1)S(1)} %copy-done.5, ...), custom_call_target="tpu_custom_call" | custom-call | flops 50331648 | bytes 3369996 | tf_op jit(solution)/shard_map/attend/pallas_call | solution.py:303
  16.3 1.7 %collective-permute-start.3 = (f32[8,256]{1,0:T(8,128)S(1)}, f32[8,256]{1,0:T(8,128)S(1)}, u32[]{:S(2)}, u32[]{:S(2)}) collective-permute-start(f32[8,256]{1,0:T(8,128)S(1)} %get-tuple-element.25), channel_id=1, source_target_pairs={{0,1},{1,0},{2,3},{3,2},{4,5},{5,4},{6,7},{7,6},{8,9},{9,8},{10,11... | collective-permute-start | bytes 24584 | tf_op jit(solution)/shard_map/ppermute | solution.py:317
  18.0 2.0 %collective-permute-done.3 = f32[8,256]{1,0:T(8,128)S(1)} collective-permute-done((f32[8,256]{1,0:T(8,128)S(1)}, f32[8,256]{1,0:T(8,128)S(1)}, u32[]{:S(2)}, u32[]{:S(2)}) %collective-permute-start.3) | collective-permute-done | bytes 8224 | tf_op jit(solution)/shard_map/ppermute | solution.py:317
  20.0 1.8 %collective-permute-start.4 = (f32[8,256]{1,0:T(8,128)S(1)}, f32[8,256]{1,0:T(8,128)S(1)}, u32[]{:S(2)}, u32[]{:S(2)}) collective-permute-start(f32[8,256]{1,0:T(8,128)S(1)} %add.3.refs_0_), channel_id=1, source_target_pairs={{0,2},{1,3},{2,0},{3,1},{4,6},{5,7},{6,4},{7,5},{8,10},{9,11},{10,... | collective-permute-start | bytes 24584 | tf_op jit(solution)/shard_map/ppermute | solution.py:317
  21.8 2.6 %collective-permute-start.5 = (f32[8,256]{1,0:T(8,128)S(1)}, f32[8,256]{1,0:T(8,128)S(1)}, u32[]{:S(2)}, u32[]{:S(2)}) collective-permute-start(f32[8,256]{1,0:T(8,128)S(1)} %add.3.refs_0_), channel_id=1, source_target_pairs={{0,4},{1,5},{2,6},{3,7},{4,0},{5,1},{6,2},{7,3},{8,12},{9,13},{10,... | collective-permute-start | bytes 24584 | tf_op jit(solution)/shard_map/ppermute | solution.py:317
  24.4 0.0 collective-permute-start.6
  24.4 2.0 %collective-permute-done.5.refs_2_ = f32[8,256]{1,0:T(8,128)S(1)} collective-permute-done((f32[8,256]{1,0:T(8,128)S(1)}, f32[8,256]{1,0:T(8,128)S(1)}, u32[]{:S(2)}, u32[]{:S(2)}) %collective-permute-start.5) | collective-permute-done | bytes 8224 | tf_op jit(solution)/shard_map/ppermute | solution.py:317
  26.3 3.5 %collective-permute-done.6.refs_3_ = f32[8,256]{1,0:T(8,128)S(1)} collective-permute-done((f32[8,256]{1,0:T(8,128)S(1)}, f32[8,256]{1,0:T(8,128)S(1)}, u32[]{:S(2)}, u32[]{:S(2)}) %collective-permute-start.6) | collective-permute-done | bytes 8224 | tf_op jit(solution)/shard_map/ppermute | solution.py:317
  29.8 1.3 %grad.1 = (bf16[768,256]{1,0:T(8,128)(2,1)S(1)}, f32[8,256]{1,0:T(8,128)S(1)}, f32[264,128]{1,0:T(8,128)S(1)}, f32[2,2,128,128]{3,2,1,0:T(8,128)S(1)}) custom-call(s32[2]{0:T(128)S(1)} %copy-done.8, s32[6,128]{1,0:T(8,128)S(1)} %bitcast.5, bf16[768,256]{1,0:T(8,128)(2,1)S(1)} %copy-done, bf16[768,256]{1,0:T(8,128)(2,1)S(1)} %copy-done.5, ...), custom_call_target="tpu_custom_call" | custom-call | flops 50331648 | bytes 2407432 | tf_op jit(solution)/shard_map/grad/pallas_call | solution.py:303
  31.1 1.6 %collective-permute-start.7 = (f32[264,128]{1,0:T(8,128)S(1)}, f32[264,128]{1,0:T(8,128)S(1)}, u32[]{:S(2)}, u32[]{:S(2)}) collective-permute-start(f32[264,128]{1,0:T(8,128)S(1)} %get-tuple-element.35.refs_0_), channel_id=1, source_target_pairs={{0,16},{8,24},{16,0},{24,8},{1,17},{9,25},{17,1},{25,9},{2,18},{10... | collective-permute-start | bytes 405512 | tf_op jit(solution)/shard_map/ppermute | solution.py:317
  32.7 3.5 %collective-permute-done.7.refs_1_ = f32[264,128]{1,0:T(8,128)S(1)} collective-permute-done((f32[264,128]{1,0:T(8,128)S(1)}, f32[264,128]{1,0:T(8,128)S(1)}, u32[]{:S(2)}, u32[]{:S(2)}) %collective-permute-start.7) | collective-permute-done | bytes 135200 | tf_op jit(solution)/shard_map/ppermute | solution.py:317
  36.1 3.6 %inner_grads.1 = (bf16[768,256]{1,0:T(8,128)(2,1)}, bf16[768,256]{1,0:T(8,128)(2,1)}, f32[768,256]{1,0:T(8,128)S(1)}, f32[768,256]{1,0:T(8,128)S(1)}) custom-call(s32[2]{0:T(128)S(1)} %copy-done.8, s32[6,128]{1,0:T(8,128)S(1)} %bitcast.6, bf16[768,256]{1,0:T(8,128)(2,1)S(1)} %copy-done, bf16[768,256]{1,0:T(8,128)(2,1)S(1)} %copy-done.2, ...), custom_call_target="tpu_custom_call" | custom-call | flops 452984832 | bytes 5712904 | tf_op jit(solution)/shard_map/inner_grads/pallas_call | solution.py:303
  39.7 2.1 %outer_grads.1 = (bf16[768,256]{1,0:T(8,128)(2,1)}, bf16[768,256]{1,0:T(8,128)(2,1)}) custom-call(s32[2]{0:T(128)S(1)} %copy-done.8, s32[1]{0:T(128)} %bitcast.1.place_ref, s32[6,128]{1,0:T(8,128)S(1)} %bitcast.7, bf16[768,256]{1,0:T(8,128)(2,1)S(1)} %copy-done.2, bf16[768,256]{1,0:T(8,128)(2,1)S(1)} %copy-done.4, ...), custom_call_target="tpu_custom_call" | custom-call | flops 100663296 | bytes 3951628 | tf_op jit(solution)/shard_map/outer_grads/pallas_call | solution.py:303
  (21 shorter events, 0.0 us)
Async XLA Ops:
  0.6 0.7 %copy-start.8 = (s32[2]{0:T(128)S(1)}, s32[2]{0:T(128)}, u32[]{:S(2)}) copy-start(s32[2]{0:T(128)} %code_ref.11) | copy-start | bytes 28
  1.3 1.0 %copy-start.1 = (bf16[768,256]{1,0:T(8,128)(2,1)S(1)}, bf16[768,256]{1,0:T(8,128)(2,1)}, u32[]{:S(2)}) copy-start(bf16[768,256]{1,0:T(8,128)(2,1)} %k_ref.7) | copy-start | bytes 1179652
  2.3 1.0 %copy-start.3 = (bf16[768,256]{1,0:T(8,128)(2,1)S(1)}, bf16[768,256]{1,0:T(8,128)(2,1)}, u32[]{:S(2)}) copy-start(bf16[768,256]{1,0:T(8,128)(2,1)} %v_ref.7) | copy-start | bytes 1179652
  3.3 0.7 %copy-start.6 = (s32[768]{0:T(1024)S(1)}, s32[768]{0:T(1024)}, u32[]{:S(2)}) copy-start(s32[768]{0:T(1024)} %param.11) | copy-start | bytes 9220
  4.0 7.6 %copy-start = (bf16[768,256]{1,0:T(8,128)(2,1)S(1)}, bf16[768,256]{1,0:T(8,128)(2,1)}, u32[]{:S(2)}) copy-start(bf16[768,256]{1,0:T(8,128)(2,1)} %q_ref.7) | copy-start | bytes 1179652
  4.0 7.6 %copy-start.2 = (bf16[768,256]{1,0:T(8,128)(2,1)S(1)}, bf16[768,256]{1,0:T(8,128)(2,1)}, u32[]{:S(2)}) copy-start(bf16[768,256]{1,0:T(8,128)(2,1)} %k_ref.7) | copy-start | bytes 1179652
  4.9 6.6 %copy-start.7 = (s32[768]{0:T(1024)S(1)}, s32[768]{0:T(1024)}, u32[]{:S(2)}) copy-start(s32[768]{0:T(1024)} %param.11) | copy-start | bytes 9220
  4.9 6.6 %collective-permute-start = (f32[264,128]{1,0:T(8,128)S(1)}, f32[264,128]{1,0:T(8,128)S(1)}, u32[]{:S(2)}, u32[]{:S(2)}) collective-permute-start(f32[264,128]{1,0:T(8,128)S(1)} %get-tuple-element.23.refs_0_), channel_id=1, source_target_pairs={{0,16},{8,24},{16,0},{24,8},{1,17},{9,25},{17,1},{25,9},{2,18},{10... | collective-permute-start | bytes 405512 | tf_op jit(solution)/shard_map/ppermute | solution.py:317
  8.0 6.3 %collective-permute-start.1 = (f32[264,128]{1,0:T(8,128)S(1)}, f32[264,128]{1,0:T(8,128)S(1)}, u32[]{:S(2)}, u32[]{:S(2)}) collective-permute-start(f32[264,128]{1,0:T(8,128)S(1)} %get-tuple-element.23.refs_0_), channel_id=1, source_target_pairs={{0,8},{8,0},{16,24},{24,16},{1,9},{9,1},{17,25},{25,17},{2,10},{10... | collective-permute-start | bytes 405512 | tf_op jit(solution)/shard_map/ppermute | solution.py:317
  11.5 2.8 %collective-permute-start.2 = (f32[264,128]{1,0:T(8,128)S(1)}, f32[264,128]{1,0:T(8,128)S(1)}, u32[]{:S(2)}, u32[]{:S(2)}) collective-permute-start(f32[264,128]{1,0:T(8,128)S(1)} %collective-permute-done.refs_1_), channel_id=1, source_target_pairs={{0,8},{8,0},{16,24},{24,16},{1,9},{9,1},{17,25},{25,17},{2,10},{10... | collective-permute-start | bytes 405512 | tf_op jit(solution)/shard_map/ppermute | solution.py:317
  11.6 1.0 %copy-start.4 = (bf16[768,256]{1,0:T(8,128)(2,1)S(1)}, bf16[768,256]{1,0:T(8,128)(2,1)}, u32[]{:S(2)}) copy-start(bf16[768,256]{1,0:T(8,128)(2,1)} %v_ref.7) | copy-start | bytes 1179652
  12.6 1.8 %copy-start.5 = (bf16[768,256]{1,0:T(8,128)(2,1)S(1)}, bf16[768,256]{1,0:T(8,128)(2,1)}, u32[]{:S(2)}) copy-start(bf16[768,256]{1,0:T(8,128)(2,1)} %cot_ref.3) | copy-start | bytes 1179652
  16.3 3.7 %collective-permute-start.3 = (f32[8,256]{1,0:T(8,128)S(1)}, f32[8,256]{1,0:T(8,128)S(1)}, u32[]{:S(2)}, u32[]{:S(2)}) collective-permute-start(f32[8,256]{1,0:T(8,128)S(1)} %get-tuple-element.25), channel_id=1, source_target_pairs={{0,1},{1,0},{2,3},{3,2},{4,5},{5,4},{6,7},{7,6},{8,9},{9,8},{10,11... | collective-permute-start | bytes 24584 | tf_op jit(solution)/shard_map/ppermute | solution.py:317
  20.0 4.4 %collective-permute-start.4 = (f32[8,256]{1,0:T(8,128)S(1)}, f32[8,256]{1,0:T(8,128)S(1)}, u32[]{:S(2)}, u32[]{:S(2)}) collective-permute-start(f32[8,256]{1,0:T(8,128)S(1)} %add.3.refs_0_), channel_id=1, source_target_pairs={{0,2},{1,3},{2,0},{3,1},{4,6},{5,7},{6,4},{7,5},{8,10},{9,11},{10,... | collective-permute-start | bytes 24584 | tf_op jit(solution)/shard_map/ppermute | solution.py:317
  21.8 4.5 %collective-permute-start.5 = (f32[8,256]{1,0:T(8,128)S(1)}, f32[8,256]{1,0:T(8,128)S(1)}, u32[]{:S(2)}, u32[]{:S(2)}) collective-permute-start(f32[8,256]{1,0:T(8,128)S(1)} %add.3.refs_0_), channel_id=1, source_target_pairs={{0,4},{1,5},{2,6},{3,7},{4,0},{5,1},{6,2},{7,3},{8,12},{9,13},{10,... | collective-permute-start | bytes 24584 | tf_op jit(solution)/shard_map/ppermute | solution.py:317
  24.4 5.4 %collective-permute-start.6 = (f32[8,256]{1,0:T(8,128)S(1)}, f32[8,256]{1,0:T(8,128)S(1)}, u32[]{:S(2)}, u32[]{:S(2)}) collective-permute-start(f32[8,256]{1,0:T(8,128)S(1)} %add.3.refs_0_), channel_id=1, source_target_pairs={{0,6},{1,7},{2,4},{3,5},{4,2},{5,3},{6,0},{7,1},{8,14},{9,15},{10,... | collective-permute-start | bytes 24584 | tf_op jit(solution)/shard_map/ppermute | solution.py:317
  31.1 5.1 %collective-permute-start.7 = (f32[264,128]{1,0:T(8,128)S(1)}, f32[264,128]{1,0:T(8,128)S(1)}, u32[]{:S(2)}, u32[]{:S(2)}) collective-permute-start(f32[264,128]{1,0:T(8,128)S(1)} %get-tuple-element.35.refs_0_), channel_id=1, source_target_pairs={{0,16},{8,24},{16,0},{24,8},{1,17},{9,25},{17,1},{25,9},{2,18},{10... | collective-permute-start | bytes 405512 | tf_op jit(solution)/shard_map/ppermute | solution.py:317
  32.7 7.1 %collective-permute-start.8 = (f32[264,128]{1,0:T(8,128)S(1)}, f32[264,128]{1,0:T(8,128)S(1)}, u32[]{:S(2)}, u32[]{:S(2)}) collective-permute-start(f32[264,128]{1,0:T(8,128)S(1)} %get-tuple-element.35.refs_0_), channel_id=1, source_target_pairs={{0,8},{8,0},{16,24},{24,16},{1,9},{9,1},{17,25},{25,17},{2,10},{10... | collective-permute-start | bytes 405512 | tf_op jit(solution)/shard_map/ppermute | solution.py:317
  36.1 3.6 %collective-permute-start.9 = (f32[264,128]{1,0:T(8,128)S(1)}, f32[264,128]{1,0:T(8,128)S(1)}, u32[]{:S(2)}, u32[]{:S(2)}) collective-permute-start(f32[264,128]{1,0:T(8,128)S(1)} %collective-permute-done.7.refs_1_), channel_id=1, source_target_pairs={{0,8},{8,0},{16,24},{24,16},{1,9},{9,1},{17,25},{25,17},{2,10},{10... | collective-permute-start | bytes 405512 | tf_op jit(solution)/shard_map/ppermute | solution.py:317

commit v2 on v1

v2 whole, which is shorter than its diff:
```python
import functools
import math

import jax
import jax.numpy as jnp
from jax import lax
from jax.experimental import pallas as pl
from jax.experimental.pallas import tpu as pltpu
from jax.sharding import PartitionSpec as P

BLK = 256
LANES = 128
LOG_TWO = math.log(2.0)
EPSILON = 1e-06
F32 = jnp.float32
BF16 = jnp.bfloat16

NN = (((1,), (0,)), ((), ()))
NT = (((1,), (1,)), ((), ()))
TN = (((0,), (0,)), ((), ()))


def mm(a, b, dims=NN):
    return lax.dot_general(a, b, dims, preferred_element_type=F32)


def iota(shape, axis):
    return lax.broadcasted_iota(jnp.int32, shape, axis)


def up8(n):
    return -(-n // 8) * 8


def halves(x):
    head = x.astype(BF16)
    return head, (x - head.astype(F32)).astype(BF16)


ROWS = ("growth", "beyond", "decay", "total", "count", "rate")


def factor_rows(bnd_ref, code_ref, blocks, heads):
    rows = up8(blocks * heads)
    per = BLK // LANES
    bnd = bnd_ref[...].astype(F32)
    parts = []
    for b in range(blocks):
        row = jnp.concatenate([bnd[b * per + i : b * per + i + 1] for i in range(per)], axis=1)
        parts += [row] * heads
    if rows > blocks * heads:
        parts.append(jnp.zeros((rows - blocks * heads, BLK), F32))
    marks = jnp.concatenate(parts, axis=0).astype(BF16)
    upper = (iota((BLK, BLK), 0) <= iota((BLK, BLK), 1)).astype(F32).astype(BF16)
    count = mm(marks, upper)
    count_all = mm(marks, jnp.ones((BLK, BLK), BF16))
    which = iota((rows, BLK), 0)
    code = jnp.zeros((rows, BLK), F32)
    for h in range(heads):
        code = jnp.where(which % heads == h, code_ref[h].astype(F32), code)
    rate = jnp.log1p(code * -(2.0 ** (-20)))
    place = (iota((rows, BLK), 1) + 1).astype(F32)
    level = rate * place - LOG_TWO * count
    total = rate * float(BLK) - LOG_TWO * count_all
    return jnp.exp(level), jnp.exp(total - level), jnp.exp(total), total, count, rate


class Factors:
    def __init__(self, ref, blocks, heads):
        self.ref, self.blocks, self.heads, self.rows = ref, blocks, heads, up8(blocks * heads)

    def all(self, name):
        at = ROWS.index(name) * self.rows
        return self.ref[at : at + self.rows, :]

    def row(self, name, b, h, lanes=BLK):
        at = ROWS.index(name) * self.rows + b * self.heads + h
        return self.ref[at : at + 1, :lanes]

    def device_total(self, h):
        return sum(self.row("total", b, h, LANES) for b in range(self.blocks))

    def decays(self, b):
        pick = (iota((self.rows, BLK), 0) == b * self.heads).astype(F32).astype(BF16)
        count_i = mm(self.all("count").astype(BF16), pick, TN)
        halved = LOG_TWO * (count_i - self.row("count", b, 0))
        apart = iota((BLK, BLK), 0) - iota((BLK, BLK), 1)
        causal = apart >= 0
        steps = apart.astype(F32)
        return causal, [
            jnp.exp(jnp.where(causal, self.row("rate", b, h) * steps - halved, 0.0))
            for h in range(self.heads)
        ]


def spread(a, wanted, width):
    head, rest = halves(a)
    both = jnp.concatenate([head.astype(F32), rest.astype(F32)], axis=0).T.astype(BF16)
    rows = a.shape[0]
    result = []
    for some in wanted:
        lane, row = iota((2 * rows, width), 1), iota((2 * rows, width), 0) % rows
        pick = jnp.zeros((2 * rows, width), F32)
        for i, r in enumerate(some):
            share = lane // (width // len(some)) == i
            pick = jnp.where(jnp.logical_and(share, row == r), 1.0, pick)
        result.append(mm(both, pick.astype(BF16)))
    return result


def incoming(payloads, place, masks, h, head_size, heads, reverse):
    at = heads * head_size + h
    totals = [p[at : at + 1, :] for p in payloads]
    sources = [place ^ m for m in masks]

    def before(a, b):
        return a > b if reverse else a < b

    result = jnp.zeros((head_size, head_size), F32)
    for i, m in enumerate(masks):
        if m == 0:
            continue
        inner = jnp.zeros_like(totals[0])
        for j, other in enumerate(masks):
            if other in (0, m):
                continue
            between = jnp.logical_and(before(sources[i], sources[j]), before(sources[j], place))
            inner = inner + jnp.where(between, totals[j], 0.0)
        weight = jnp.where(before(sources[i], place), jnp.exp(inner), 0.0)
        result = result + weight * payloads[i][h * head_size : (h + 1) * head_size, :]
    return result


def store_totals(payload_ref, fac, head_size):
    rest = [fac.device_total(h) for h in range(fac.heads)]
    pad = up8(fac.heads) - fac.heads
    if pad:
        rest.append(jnp.zeros((pad, LANES), F32))
    payload_ref[fac.heads * head_size :, :] = jnp.concatenate(rest, axis=0)


def block(ref, b, h, e):
    return ref[b * BLK : (b + 1) * BLK, h * e : (h + 1) * e]


def states_kernel(
    dims, code_in, bnd_in, q_in, k_in, v_in, cot_in,
    payload_ref, local_ref, factors_ref, q_ref, k_ref, v_ref, cot_ref, code_ref, bnd_ref, sems,
):
    nb, heads, e = dims
    pairs = (
        (code_in, code_ref), (bnd_in, bnd_ref), (k_in, k_ref), (v_in, v_ref), (q_in, q_ref), (cot_in, cot_ref),
    )
    copies = [pltpu.make_async_copy(s, d, sems.at[i]) for i, (s, d) in enumerate(pairs)]
    for c in copies:
        c.start()
    copies[0].wait()
    copies[1].wait()
    made = factor_rows(bnd_ref, code_ref, nb, heads)
    rows = up8(nb * heads)
    for i, a in enumerate(made):
        factors_ref[i * rows : (i + 1) * rows, :] = a
    fac = Factors(factors_ref, nb, heads)
    store_totals(payload_ref, fac, e)
    copies[2].wait()
    copies[3].wait()
    for h in range(heads):
        running = None
        for b in range(nb):
            scaled = (block(k_ref, b, h, e).T.astype(F32) * fac.row("beyond", b, h)).astype(BF16)
            term = mm(scaled, block(v_ref, b, h, e))
            running = term if running is None else fac.row("decay", b, h, e) * running + term
            if b < nb - 1:
                local_ref[b, h] = running
        payload_ref[h * e : (h + 1) * e, :] = running
    copies[4].wait()
    copies[5].wait()


def within_kernel(dims, factors_ref, q_ref, k_ref, v_ref, w_ref, within_ref, growth_ref, beyond_ref):
    nb, heads, e = dims
    fac = Factors(factors_ref, nb, heads)
    wanted = [[b * heads + h for h in range(heads)] for b in range(nb)]
    for name, ref in (("growth", growth_ref), ("beyond", beyond_ref)):
        for b, a in enumerate(spread(fac.all(name), wanted, heads * e)):
            ref[b * BLK : (b + 1) * BLK, :] = a
    for b in range(nb):
        causal, decays = fac.decays(b)
        for h in range(heads):
            scores = mm(block(q_ref, b, h, e), block(k_ref, b, h, e), NT)
            weights = jnp.where(causal, scores * decays[h], 0.0).astype(BF16)
            w_ref[b, h] = weights
            within_ref[b * BLK : (b + 1) * BLK, h * e : (h + 1) * e] = mm(
                weights, block(v_ref, b, h, e)
            )


def row_sums(a):
    width = a.shape[1]
    narrow = sum(a[:, i : i + LANES] for i in range(0, width, LANES))
    return jnp.sum(narrow.T, axis=0, keepdims=True)


def attend_kernel(
    dims, masks, factors_ref, q_ref, cot_ref, within_ref, growth_ref, local_ref, *refs
):
    payloads, (held_ref, att_ref, sums_ref) = refs[: len(masks)], refs[len(masks) :]
    nb, heads, e = dims
    fac = Factors(factors_ref, nb, heads)
    for h in range(heads):
        arrived = incoming(payloads, lax.axis_index("ctx"), masks, h, e, heads, False)
        ahead = jnp.zeros((1, e), F32)
        for b in range(nb):
            state = jnp.exp(ahead) * arrived
            if b:
                state = state + local_ref[b - 1, h]
            ahead = ahead + fac.row("total", b, h, e)
            held_ref[b, h] = state.astype(BF16)
    squares, crosses = [], []
    for b in range(nb):
        rows = slice(b * BLK, (b + 1) * BLK)
        carried = jnp.concatenate(
            [mm(block(q_ref, b, h, e), held_ref[b, h]) for h in range(heads)], axis=1
        )
        att = within_ref[rows, :] + growth_ref[rows, :] * carried
        att_ref[rows, :] = att
        squares.append(row_sums(att * att))
        crosses.append(row_sums(att * cot_ref[rows, :].astype(F32)))
    parts = squares + crosses
    if up8(2 * nb) > 2 * nb:
        parts.append(jnp.zeros((up8(2 * nb) - 2 * nb, BLK), F32))
    sums_ref[...] = jnp.concatenate(parts, axis=0)


def grad_kernel(dims, full_width, parts, factors_ref, q_ref, cot_ref, att_ref, *refs):
    sums_refs, (g_ref, scale_ref, payload_ref, local_ref) = refs[:parts], refs[parts:]
    nb, heads, e = dims
    fac = Factors(factors_ref, nb, heads)
    sums = sum(ref[...] for ref in sums_refs)
    squares = jnp.where(iota(sums.shape, 0) < nb, sums, 0.0)
    scale = lax.rsqrt(squares / full_width + EPSILON)
    scale_ref[...] = scale
    squared = scale * scale
    lean = jnp.concatenate([squared[:nb], squared[:nb], squared[2 * nb :]], axis=0) * sums / full_width
    factors = jnp.where(iota(sums.shape, 0) < nb, scale, lean)
    columns = spread(factors, [[r] for r in range(2 * nb)], heads * e)
    for b in range(nb):
        rows = slice(b * BLK, (b + 1) * BLK)
        g_ref[rows, :] = (
            columns[b] * (cot_ref[rows, :].astype(F32) - att_ref[rows, :] * columns[nb + b])
        ).astype(BF16)
    for h in range(heads):
        running = None
        for b in reversed(range(nb)):
            lifted = (block(q_ref, b, h, e).T.astype(F32) * fac.row("growth", b, h)).astype(BF16)
            term = mm(lifted, block(g_ref, b, h, e))
            running = term if running is None else fac.row("decay", b, h, e) * running + term
            if b:
                local_ref[b - 1, h] = running
        payload_ref[h * e : (h + 1) * e, :] = running
    store_totals(payload_ref, fac, e)


def inner_grads_kernel(
    dims, factors_ref, q_ref, k_ref, v_ref, g_ref, w_ref, held_ref, att_ref, growth_ref, scale_ref,
    out_hbm, gq_hbm, gk_ref, gv_ref, out_ref, gq_ref, sems,
):
    nb, heads, e = dims
    fac = Factors(factors_ref, nb, heads)
    scale = spread(scale_ref[...], [[b] for b in range(nb)], heads * e)
    copies = []
    for b in range(nb):
        rows = slice(b * BLK, (b + 1) * BLK)
        out_ref[rows, :] = (att_ref[rows, :] * scale[b]).astype(BF16)
        copies.append(
            pltpu.make_async_copy(out_ref.at[rows], out_hbm.at[rows], sems.at[2 * b])
        )
        copies[-1].start()
        causal, decays = fac.decays(b)
        for h in range(heads):
            cols = slice(h * e, (h + 1) * e)
            g = block(g_ref, b, h, e)
            scores = mm(g, block(v_ref, b, h, e), NT)
            gw = jnp.where(causal, scores * decays[h], 0.0).astype(BF16)
            gq = mm(gw, block(k_ref, b, h, e)) + growth_ref[rows, cols] * mm(g, held_ref[b, h], NT)
            gq_ref[rows, cols] = gq.astype(BF16)
            gk_ref[rows, cols] = mm(gw, block(q_ref, b, h, e), TN)
            gv_ref[rows, cols] = mm(w_ref[b, h], g, TN)
        copies.append(
            pltpu.make_async_copy(gq_ref.at[rows], gq_hbm.at[rows], sems.at[2 * b + 1])
        )
        copies[-1].start()
    for c in copies:
        c.wait()


def outer_grads_kernel(
    dims, masks, factors_ref, k_ref, v_ref, gk_part_ref, gv_part_ref, beyond_ref, local_ref, *refs
):
    payloads, (gk_hbm, gv_hbm, gk_ref, gv_ref, sems) = refs[: len(masks)], refs[len(masks) :]
    nb, heads, e = dims
    fac = Factors(factors_ref, nb, heads)
    arrived = [incoming(payloads, lax.axis_index("ctx"), masks, h, e, heads, True) for h in range(heads)]
    behind = [jnp.zeros((1, e), F32) for h in range(heads)]
    copies = []
    for b in reversed(range(nb)):
        rows = slice(b * BLK, (b + 1) * BLK)
        for h in range(heads):
            cols = slice(h * e, (h + 1) * e)
            state = jnp.exp(behind[h]) * arrived[h]
            if b < nb - 1:
                state = state + local_ref[b, h]
            behind[h] = behind[h] + fac.row("total", b, h, e)
            held = state.astype(BF16)
            far = beyond_ref[rows, cols]
            gk = gk_part_ref[rows, cols] + far * mm(block(v_ref, b, h, e), held, NT)
            gk_ref[rows, cols] = gk.astype(BF16)
            gv = gv_part_ref[rows, cols] + far * mm(block(k_ref, b, h, e), held)
            gv_ref[rows, cols] = gv.astype(BF16)
        for i, (s, d) in enumerate(((gk_ref, gk_hbm), (gv_ref, gv_hbm))):
            copies.append(pltpu.make_async_copy(s.at[rows], d.at[rows], sems.at[2 * b + i]))
            copies[-1].start()
    for c in copies:
        c.wait()


def call(kernel, name, args, outs, flops, hbm_in=False, hbm_outs=0, scratch=()):
    traffic = sum(a.size * a.dtype.itemsize for a in args) + sum(
        math.prod(s) * jnp.dtype(d).itemsize for s, d in outs
    )
    hbm = pl.BlockSpec(memory_space=pltpu.HBM)
    vmem, smem = pl.BlockSpec(memory_space=pltpu.VMEM), pl.BlockSpec(memory_space=pltpu.SMEM)
    if hbm_in:
        args = [pltpu.with_memory_space_constraint(a, pltpu.HBM) for a in args]
    return pl.pallas_call(
        kernel,
        out_shape=[(pltpu.HBM if i < hbm_outs else pltpu.VMEM)(s, d) for i, (s, d) in enumerate(outs)],
        in_specs=[hbm if hbm_in else smem if a.ndim == 1 else vmem for a in args],
        out_specs=[hbm if i < hbm_outs else vmem for i in range(len(outs))],
        scratch_shapes=scratch,
        compiler_params=pltpu.CompilerParams(vmem_limit_bytes=16 * 2**20),
        cost_estimate=pl.CostEstimate(flops=flops, bytes_accessed=traffic, transcendentals=0),
        name=name,
    )(*args)


def nothing(*refs):
    pass


def after(a, other):
    anywhere = pl.BlockSpec(memory_space=pltpu.VMEM)
    return pl.pallas_call(
        nothing,
        out_shape=pltpu.VMEM(a.shape, a.dtype),
        in_specs=[anywhere, anywhere],
        out_specs=anywhere,
        input_output_aliases={0: 0},
        compiler_params=pltpu.CompilerParams(vmem_limit_bytes=4 * 2**20),
        name="after",
    )(a, other)


def swap(a, axis, mask):
    return lax.ppermute(a, axis, [(i, i ^ mask) for i in range(lax.axis_size(axis))])


def gather_states(payload, work):
    bit = lax.axis_size("ctx") // 2
    first = swap(payload, "ctx", bit) if bit else payload
    done = work()
    first = after(first, done[-1])
    masks, held = ([0, bit], [payload, first]) if bit else ([0], [payload])
    bit //= 2
    while bit:
        held += [swap(a, "ctx", bit) for a in held]
        masks += [m | bit for m in masks]
        bit //= 2
    return masks, held, done


def sum_over_heads(sums):
    size = lax.axis_size("head")
    parts, bit, width = [sums], 1, 2
    while bit < size:
        own = functools.reduce(jnp.add, parts)
        width = min(width, size // bit)
        parts = [own] + [swap(own, "head", bit * i) for i in range(1, width)]
        bit, width = bit * width, 4
    return parts


def shards(queries, keys, values, cotangent, decay_code, boundaries):
    tokens, width = queries.shape
    heads = decay_code.shape[0]
    e = width // heads
    nb = tokens // BLK
    dims = (nb, heads, e)
    full_width = width * lax.axis_size("head")
    bnd = boundaries.reshape(tokens // LANES, LANES)
    payload = ((heads * e + up8(heads), LANES), F32)
    local = ((max(nb - 1, 1), heads, e, e), F32)
    narrow, wide = ((tokens, width), BF16), ((tokens, width), F32)
    stage = [pltpu.VMEM((tokens, width), BF16)] * 2 + [pltpu.SemaphoreType.DMA((2 * nb,))]
    big = 2 * tokens * heads * e * BLK
    small = 2 * tokens * heads * e * e

    state, prefix, factors, q, k, v, cot = call(
        functools.partial(states_kernel, dims), "states",
        (decay_code, bnd, queries, keys, values, cotangent),
        (payload, local, ((len(ROWS) * up8(nb * heads), BLK), F32), narrow, narrow, narrow, narrow), small,
        hbm_in=True,
        scratch=(pltpu.SMEM((heads,), jnp.int32), pltpu.VMEM(bnd.shape, jnp.int32), pltpu.SemaphoreType.DMA((6,))),
    )
    masks, states, (weights, within, growth, beyond) = gather_states(state, lambda: call(
        functools.partial(within_kernel, dims), "within", (factors, q, k, v),
        (((nb, heads, BLK, BLK), BF16), wide, wide, wide), 2 * big,
    ))
    held, attended, sums = call(
        functools.partial(attend_kernel, dims, masks), "attend",
        (factors, q, cot, within, growth, prefix, *states),
        (((nb, heads, e, e), BF16), wide, ((up8(2 * nb), BLK), F32)), small,
    )
    sums = sum_over_heads(sums)
    grad, scale, grad_state, suffix = call(
        functools.partial(grad_kernel, dims, full_width, len(sums)), "grad",
        (factors, q, cot, attended, *sums),
        (narrow, ((up8(2 * nb), BLK), F32), payload, local), small,
    )
    masks, grad_states, (output, grad_queries, gk_part, gv_part) = gather_states(grad_state, lambda: call(
        functools.partial(inner_grads_kernel, dims), "inner_grads",
        (factors, q, k, v, grad, weights, held, attended, growth, scale),
        (narrow, narrow, wide, wide), 4 * big + small, hbm_outs=2, scratch=stage,
    ))
    grad_keys, grad_values = call(
        functools.partial(outer_grads_kernel, dims, masks), "outer_grads",
        (factors, k, v, gk_part, gv_part, beyond, suffix, *grad_states),
        (narrow, narrow), 2 * small, hbm_outs=2, scratch=stage,
    )
    return output, grad_queries, grad_keys, grad_values


def solution(mesh):
    both = P("ctx", "head")
    return jax.shard_map(
        shards,
        mesh=mesh,
        in_specs=(both, both, both, both, P("head"), P("ctx")),
        out_specs=(both, both, both, both),
        check_vma=False,
    )
```

time: 42.2 us -> 31.3 us (0.74)
  local copies, waits for them, and re-layouts: 4.33 us -> 0 us
  Pallas kernels: 11.6 us -> 8.02 us
  waiting for transfers between devices: 14.5 us -> 11.6 us
    unnamed x18 -> x0, local copies, waits for them, and re-layouts: 4.33 us -> none
    pallas_call x6 -> x8, Pallas kernels: 11.6 us -> 8.02 us  [the longest x6 8.02 us: call(): pl.pallas_call(kernel, out_shape=[(pltpu.HBM if i < hbm_outs else pltpu.V...]
    ppermute x10, waiting for transfers between devices: 14.5 us -> 11.6 us  [swap(): lax.ppermute(a, axis, [(i, i ^ mask) for i in range(lax.axis_size(axis))])]
  transfers between devices with their start and end apart: 10 -> 10, of which waited for: 5 -> 7; matrix products, arithmetic and copies ran while one was open for 0% -> 0% of each run, Pallas kernels for 13% -> 13%
where the time goes in v2:
time: 31.3 us; the launch traced here: 31.1 us
  waiting for transfers between devices  11.6 us (37%)
  starting transfers between devices  10.8 us (35%)
  Pallas kernels  8.02 us (26%)
  between operations  0.68 us (2%)
    ppermute x10, waiting for transfers between devices, swap(): lax.ppermute(a, axis, [(i, i ^ mask) for i in range(lax.axis_size(axis))])  11.6 us
    ppermute x10, starting transfers between devices, swap(): lax.ppermute(a, axis, [(i, i ^ mask) for i in range(lax.axis_size(axis))])  10.8 us
    pallas_call x6, Pallas kernels, call(): pl.pallas_call(kernel, out_shape=[(pltpu.HBM if i < hbm_outs else pltpu.V...  8.02 us
  transfers between devices with their start and end apart: 10, of which 7 were waited for; matrix products, arithmetic and copies ran while one was open for 0% of the time, Pallas kernels for 13%

profile of v2, /device:TPU:0, one launch (start us, length us, event | category | flops | bytes accessed | tf_op | source)
XLA Modules:
  0.0 31.1 jit_solution(3808655022083284312)
XLA Ops:
  0.6 1.5 %states.1 = (f32[264,128]{1,0:T(8,128)S(1)}, f32[2,2,128,128]{3,2,1,0:T(8,128)S(1)}, f32[48,256]{1,0:T(8,128)S(1)}, bf16[768,256]{1,0:T(8,128)(2,1)S(1)}, bf16[7...) custom-call(s32[2]{0:T(128)} %code_in.1, s32[6,128]{1,0:T(8,128)} %bitcast.1, ...), custom_call_target="tpu_custom_call" | custom-call | flops 50331648 | bytes 3595272 | tf_op jit(solution)/shard_map/states/pallas_call | solution.py:335
  2.1 3.0 %collective-permute-start = (f32[264,128]{1,0:T(8,128)S(1)}, f32[264,128]{1,0:T(8,128)S(1)}, u32[]{:S(2)}, u32[]{:S(2)}) collective-permute-start(f32[264,128]{1,0:T(8,128)S(1)} %get-tuple-element.36.refs_0_), channel_id=1, source_target_pairs={{0,16},{8,24},{16,0},{24,8},{1,17},{9,25},{17,1},{25,9},{2,18},{10... | collective-permute-start | bytes 405512 | tf_op jit(solution)/shard_map/ppermute | solution.py:365
  5.2 0.0 collective-permute-start.1
  5.2 1.2 %within.1 = (bf16[3,2,256,256]{3,2,1,0:T(8,128)(2,1)S(1)}, f32[768,256]{1,0:T(8,128)S(1)}, f32[768,256]{1,0:T(8,128)S(1)}, f32[768,256]{1,0:T(8,128)S(1)}) custom-call(f32[48,256]{1,0:T(8,128)S(1)} %get-tuple-element.28.factors_ref, bf16[768,256]{1,0:T(8,128)(2,1)S(1)} %get-tuple-element.29.q_ref, bf16[768,256]{1,0:T(8,128)(2,1)S(1)} %get-tuple-element.30.k_ref, ...), custom_call_target="tpu_custom_call" | custom-call | flops 201326592 | bytes 4374528 | tf_op jit(solution)/shard_map/within/pallas_call | solution.py:335
  6.4 2.3 %collective-permute-done.refs_0_ = f32[264,128]{1,0:T(8,128)S(1)} collective-permute-done((f32[264,128]{1,0:T(8,128)S(1)}, f32[264,128]{1,0:T(8,128)S(1)}, u32[]{:S(2)}, u32[]{:S(2)}) %collective-permute-start) | collective-permute-done | bytes 135200 | tf_op jit(solution)/shard_map/ppermute | solution.py:365
  8.8 0.0 collective-permute-start.2
  8.8 0.0 collective-permute-done.1.refs_2_
  8.8 1.3 %collective-permute-done.2.refs_3_ = f32[264,128]{1,0:T(8,128)S(1)} collective-permute-done((f32[264,128]{1,0:T(8,128)S(1)}, f32[264,128]{1,0:T(8,128)S(1)}, u32[]{:S(2)}, u32[]{:S(2)}) %collective-permute-start.2) | collective-permute-done | bytes 135200 | tf_op jit(solution)/shard_map/ppermute | solution.py:365
  10.1 0.5 %attend.1 = (bf16[3,2,128,128]{3,2,1,0:T(8,128)(2,1)S(1)}, f32[768,256]{1,0:T(8,128)S(1)}, f32[8,256]{1,0:T(8,128)S(1)}) custom-call(f32[48,256]{1,0:T(8,128)S(1)} %get-tuple-element.28.factors_ref, bf16[768,256]{1,0:T(8,128)(2,1)S(1)} %get-tuple-element.29.q_ref, bf16[768,256]{1,0:T(8,128)(2,1)S(1)} %get-tuple-element.32.cot_ref, ...), custom_call_target="tpu_custom_call" | custom-call | flops 50331648 | bytes 4202496 | tf_op jit(solution)/shard_map/attend/pallas_call | solution.py:335
  10.7 1.8 %collective-permute-start.3 = (f32[8,256]{1,0:T(8,128)S(1)}, f32[8,256]{1,0:T(8,128)S(1)}, u32[]{:S(2)}, u32[]{:S(2)}) collective-permute-start(f32[8,256]{1,0:T(8,128)S(1)} %get-tuple-element.39), channel_id=1, source_target_pairs={{0,1},{1,0},{2,3},{3,2},{4,5},{5,4},{6,7},{7,6},{8,9},{9,8},{10,11... | collective-permute-start | bytes 24584 | tf_op jit(solution)/shard_map/ppermute | solution.py:365
  12.4 1.9 %collective-permute-done.3 = f32[8,256]{1,0:T(8,128)S(1)} collective-permute-done((f32[8,256]{1,0:T(8,128)S(1)}, f32[8,256]{1,0:T(8,128)S(1)}, u32[]{:S(2)}, u32[]{:S(2)}) %collective-permute-start.3) | collective-permute-done | bytes 8224 | tf_op jit(solution)/shard_map/ppermute | solution.py:365
  14.4 3.8 %collective-permute-start.6 = (f32[8,256]{1,0:T(8,128)S(1)}, f32[8,256]{1,0:T(8,128)S(1)}, u32[]{:S(2)}, u32[]{:S(2)}) collective-permute-start(f32[8,256]{1,0:T(8,128)S(1)} %add.3.refs_0_), channel_id=1, source_target_pairs={{0,6},{1,7},{2,4},{3,5},{4,2},{5,3},{6,0},{7,1},{8,14},{9,15},{10,... | collective-permute-start | bytes 24584 | tf_op jit(solution)/shard_map/ppermute | solution.py:365
  18.2 0.0 collective-permute-start.5
  18.2 0.6 %collective-permute-start.4 = (f32[8,256]{1,0:T(8,128)S(1)}, f32[8,256]{1,0:T(8,128)S(1)}, u32[]{:S(2)}, u32[]{:S(2)}) collective-permute-start(f32[8,256]{1,0:T(8,128)S(1)} %add.3.refs_0_), channel_id=1, source_target_pairs={{0,2},{1,3},{2,0},{3,1},{4,6},{5,7},{6,4},{7,5},{8,10},{9,11},{10,... | collective-permute-start | bytes 24584 | tf_op jit(solution)/shard_map/ppermute | solution.py:365
  18.8 1.1 %collective-permute-done.6.refs_3_ = f32[8,256]{1,0:T(8,128)S(1)} collective-permute-done((f32[8,256]{1,0:T(8,128)S(1)}, f32[8,256]{1,0:T(8,128)S(1)}, u32[]{:S(2)}, u32[]{:S(2)}) %collective-permute-start.6) | collective-permute-done | bytes 8224 | tf_op jit(solution)/shard_map/ppermute | solution.py:365
  19.8 2.9 %collective-permute-done.5.refs_2_ = f32[8,256]{1,0:T(8,128)S(1)} collective-permute-done((f32[8,256]{1,0:T(8,128)S(1)}, f32[8,256]{1,0:T(8,128)S(1)}, u32[]{:S(2)}, u32[]{:S(2)}) %collective-permute-start.5) | collective-permute-done | bytes 8224 | tf_op jit(solution)/shard_map/ppermute | solution.py:365
  22.8 0.0 collective-permute-done.4.refs_1_
  22.8 0.7 %grad.1 = (bf16[768,256]{1,0:T(8,128)(2,1)S(1)}, f32[8,256]{1,0:T(8,128)S(1)}, f32[264,128]{1,0:T(8,128)S(1)}, f32[2,2,128,128]{3,2,1,0:T(8,128)S(1)}) custom-call(f32[48,256]{1,0:T(8,128)S(1)} %get-tuple-element.28.factors_ref, bf16[768,256]{1,0:T(8,128)(2,1)S(1)} %get-tuple-element.29.q_ref, bf16[768,256]{1,0:T(8,128)(2,1)S(1)} %get-tuple-element.32.cot_ref, ...), custom_call_target="tpu_custom_call" | custom-call | flops 50331648 | bytes 2453504 | tf_op jit(solution)/shard_map/grad/pallas_call | solution.py:335
  23.5 1.6 %collective-permute-start.7 = (f32[264,128]{1,0:T(8,128)S(1)}, f32[264,128]{1,0:T(8,128)S(1)}, u32[]{:S(2)}, u32[]{:S(2)}) collective-permute-start(f32[264,128]{1,0:T(8,128)S(1)} %get-tuple-element.49.refs_0_), channel_id=1, source_target_pairs={{0,16},{8,24},{16,0},{24,8},{1,17},{9,25},{17,1},{25,9},{2,18},{10... | collective-permute-start | bytes 405512 | tf_op jit(solution)/shard_map/ppermute | solution.py:365
  25.1 2.8 %inner_grads.1 = (bf16[768,256]{1,0:T(8,128)(2,1)}, bf16[768,256]{1,0:T(8,128)(2,1)}, f32[768,256]{1,0:T(8,128)S(1)}, f32[768,256]{1,0:T(8,128)S(1)}) custom-call(f32[48,256]{1,0:T(8,128)S(1)} %get-tuple-element.28.factors_ref, bf16[768,256]{1,0:T(8,128)(2,1)S(1)} %get-tuple-element.29.q_ref, bf16[768,256]{1,0:T(8,128)(2,1)S(1)} %get-tuple-element.30.k_ref, ...), custom_call_target="tpu_custom_call" | custom-call | flops 452984832 | bytes 6545408 | tf_op jit(solution)/shard_map/inner_grads/pallas_call | solution.py:335
  27.9 0.6 %collective-permute-done.7.refs_0_ = f32[264,128]{1,0:T(8,128)S(1)} collective-permute-done((f32[264,128]{1,0:T(8,128)S(1)}, f32[264,128]{1,0:T(8,128)S(1)}, u32[]{:S(2)}, u32[]{:S(2)}) %collective-permute-start.7) | collective-permute-done | bytes 135200 | tf_op jit(solution)/shard_map/ppermute | solution.py:365
  28.6 0.0 collective-permute-done.8.refs_2_
  28.6 1.3 %collective-permute-done.9.refs_3_ = f32[264,128]{1,0:T(8,128)S(1)} collective-permute-done((f32[264,128]{1,0:T(8,128)S(1)}, f32[264,128]{1,0:T(8,128)S(1)}, u32[]{:S(2)}, u32[]{:S(2)}) %collective-permute-start.9) | collective-permute-done | bytes 135200 | tf_op jit(solution)/shard_map/ppermute | solution.py:365
  29.9 1.2 %outer_grads.1 = (bf16[768,256]{1,0:T(8,128)(2,1)}, bf16[768,256]{1,0:T(8,128)(2,1)}) custom-call(f32[48,256]{1,0:T(8,128)S(1)} %get-tuple-element.28.factors_ref, bf16[768,256]{1,0:T(8,128)(2,1)S(1)} %get-tuple-element.30.k_ref, bf16[768,256]{1,0:T(8,128)(2,1)S(1)} %get-tuple-element.31.v_ref, f32[768,256]{1,0:T(8,128)S(1)} %get-tuple-element.46.gk_part_ref, ...), custom_call_target="tpu_custom_call" | custom-call | flops 100663296 | bytes 4784128 | tf_op jit(solution)/shard_map/outer_grads/pallas_call | solution.py:335
  (5 shorter events, 0.0 us)
Async XLA Ops:
  2.1 6.6 %collective-permute-start = (f32[264,128]{1,0:T(8,128)S(1)}, f32[264,128]{1,0:T(8,128)S(1)}, u32[]{:S(2)}, u32[]{:S(2)}) collective-permute-start(f32[264,128]{1,0:T(8,128)S(1)} %get-tuple-element.36.refs_0_), channel_id=1, source_target_pairs={{0,16},{8,24},{16,0},{24,8},{1,17},{9,25},{17,1},{25,9},{2,18},{10... | collective-permute-start | bytes 405512 | tf_op jit(solution)/shard_map/ppermute | solution.py:365
  5.2 3.6 %collective-permute-start.1 = (f32[264,128]{1,0:T(8,128)S(1)}, f32[264,128]{1,0:T(8,128)S(1)}, u32[]{:S(2)}, u32[]{:S(2)}) collective-permute-start(f32[264,128]{1,0:T(8,128)S(1)} %get-tuple-element.36.refs_0_), channel_id=1, source_target_pairs={{0,8},{8,0},{16,24},{24,16},{1,9},{9,1},{17,25},{25,17},{2,10},{10... | collective-permute-start | bytes 405512 | tf_op jit(solution)/shard_map/ppermute | solution.py:365
  8.8 1.4 %collective-permute-start.2 = (f32[264,128]{1,0:T(8,128)S(1)}, f32[264,128]{1,0:T(8,128)S(1)}, u32[]{:S(2)}, u32[]{:S(2)}) collective-permute-start(f32[264,128]{1,0:T(8,128)S(1)} %after.2.refs_1_), channel_id=1, source_target_pairs={{0,8},{8,0},{16,24},{24,16},{1,9},{9,1},{17,25},{25,17},{2,10},{10... | collective-permute-start | bytes 405512 | tf_op jit(solution)/shard_map/ppermute | solution.py:365
  10.7 3.7 %collective-permute-start.3 = (f32[8,256]{1,0:T(8,128)S(1)}, f32[8,256]{1,0:T(8,128)S(1)}, u32[]{:S(2)}, u32[]{:S(2)}) collective-permute-start(f32[8,256]{1,0:T(8,128)S(1)} %get-tuple-element.39), channel_id=1, source_target_pairs={{0,1},{1,0},{2,3},{3,2},{4,5},{5,4},{6,7},{7,6},{8,9},{9,8},{10,11... | collective-permute-start | bytes 24584 | tf_op jit(solution)/shard_map/ppermute | solution.py:365
  14.4 5.5 %collective-permute-start.6 = (f32[8,256]{1,0:T(8,128)S(1)}, f32[8,256]{1,0:T(8,128)S(1)}, u32[]{:S(2)}, u32[]{:S(2)}) collective-permute-start(f32[8,256]{1,0:T(8,128)S(1)} %add.3.refs_0_), channel_id=1, source_target_pairs={{0,6},{1,7},{2,4},{3,5},{4,2},{5,3},{6,0},{7,1},{8,14},{9,15},{10,... | collective-permute-start | bytes 24584 | tf_op jit(solution)/shard_map/ppermute | solution.py:365
  18.2 4.5 %collective-permute-start.5 = (f32[8,256]{1,0:T(8,128)S(1)}, f32[8,256]{1,0:T(8,128)S(1)}, u32[]{:S(2)}, u32[]{:S(2)}) collective-permute-start(f32[8,256]{1,0:T(8,128)S(1)} %add.3.refs_0_), channel_id=1, source_target_pairs={{0,4},{1,5},{2,6},{3,7},{4,0},{5,1},{6,2},{7,3},{8,12},{9,13},{10,... | collective-permute-start | bytes 24584 | tf_op jit(solution)/shard_map/ppermute | solution.py:365
  18.2 4.5 %collective-permute-start.4 = (f32[8,256]{1,0:T(8,128)S(1)}, f32[8,256]{1,0:T(8,128)S(1)}, u32[]{:S(2)}, u32[]{:S(2)}) collective-permute-start(f32[8,256]{1,0:T(8,128)S(1)} %add.3.refs_0_), channel_id=1, source_target_pairs={{0,2},{1,3},{2,0},{3,1},{4,6},{5,7},{6,4},{7,5},{8,10},{9,11},{10,... | collective-permute-start | bytes 24584 | tf_op jit(solution)/shard_map/ppermute | solution.py:365
  23.5 5.1 %collective-permute-start.7 = (f32[264,128]{1,0:T(8,128)S(1)}, f32[264,128]{1,0:T(8,128)S(1)}, u32[]{:S(2)}, u32[]{:S(2)}) collective-permute-start(f32[264,128]{1,0:T(8,128)S(1)} %get-tuple-element.49.refs_0_), channel_id=1, source_target_pairs={{0,16},{8,24},{16,0},{24,8},{1,17},{9,25},{17,1},{25,9},{2,18},{10... | collective-permute-start | bytes 405512 | tf_op jit(solution)/shard_map/ppermute | solution.py:365
  25.1 3.5 %collective-permute-start.8 = (f32[264,128]{1,0:T(8,128)S(1)}, f32[264,128]{1,0:T(8,128)S(1)}, u32[]{:S(2)}, u32[]{:S(2)}) collective-permute-start(f32[264,128]{1,0:T(8,128)S(1)} %get-tuple-element.49.refs_0_), channel_id=1, source_target_pairs={{0,8},{8,0},{16,24},{24,16},{1,9},{9,1},{17,25},{25,17},{2,10},{10... | collective-permute-start | bytes 405512 | tf_op jit(solution)/shard_map/ppermute | solution.py:365
  28.6 1.4 %collective-permute-start.9 = (f32[264,128]{1,0:T(8,128)S(1)}, f32[264,128]{1,0:T(8,128)S(1)}, u32[]{:S(2)}, u32[]{:S(2)}) collective-permute-start(f32[264,128]{1,0:T(8,128)S(1)} %after.3.refs_1_), channel_id=1, source_target_pairs={{0,8},{8,0},{16,24},{24,16},{1,9},{9,1},{17,25},{25,17},{2,10},{10... | collective-permute-start | bytes 405512 | tf_op jit(solution)/shard_map/ppermute | solution.py:365

commit v3 on v2

--- a/solution.py
+++ b/solution.py
@@ -144,26 +144,28 @@
 
 
 def states_kernel(
-    dims, code_in, bnd_in, q_in, k_in, v_in, cot_in,
-    payload_ref, local_ref, factors_ref, q_ref, k_ref, v_ref, cot_ref, code_ref, bnd_ref, sems,
+    dims, code_in, bnd_in, k_in, v_in,
+    payload_ref, local_ref, factors_ref, k_ref, v_ref, code_ref, bnd_ref, sems,
 ):
     nb, heads, e = dims
-    pairs = (
-        (code_in, code_ref), (bnd_in, bnd_ref), (k_in, k_ref), (v_in, v_ref), (q_in, q_ref), (cot_in, cot_ref),
-    )
-    copies = [pltpu.make_async_copy(s, d, sems.at[i]) for i, (s, d) in enumerate(pairs)]
-    for c in copies:
+    fetch = [
+        pltpu.make_async_copy(s, d, sems.at[i])
+        for i, (s, d) in enumerate(((code_in, code_ref), (bnd_in, bnd_ref)))
+    ]
+    for s, d in ((k_in, k_ref), (v_in, v_ref)):
+        fetch.append(pltpu.make_async_copy(s, d, sems.at[len(fetch)]))
+    for c in fetch:
         c.start()
-    copies[0].wait()
-    copies[1].wait()
+    fetch[0].wait()
+    fetch[1].wait()
     made = factor_rows(bnd_ref, code_ref, nb, heads)
     rows = up8(nb * heads)
     for i, a in enumerate(made):
         factors_ref[i * rows : (i + 1) * rows, :] = a
     fac = Factors(factors_ref, nb, heads)
     store_totals(payload_ref, fac, e)
-    copies[2].wait()
-    copies[3].wait()
+    fetch[2].wait()
+    fetch[3].wait()
     for h in range(heads):
         running = None
         for b in range(nb):
@@ -173,26 +175,37 @@
             if b < nb - 1:
                 local_ref[b, h] = running
         payload_ref[h * e : (h + 1) * e, :] = running
-    copies[4].wait()
-    copies[5].wait()
-
-
-def within_kernel(dims, factors_ref, q_ref, k_ref, v_ref, w_ref, within_ref, growth_ref, beyond_ref):
-    nb, heads, e = dims
+
+
+def within_kernel(
+    dims, q_in, cot_in, factors_ref, k_ref, v_ref,
+    w_ref, within_ref, growth_ref, beyond_ref, lifted_ref, q_ref, cot_ref, sems,
+):
+    nb, heads, e = dims
+    fetch = [
+        pltpu.make_async_copy(s, d, sems.at[i])
+        for i, (s, d) in enumerate(((q_in, q_ref), (cot_in, cot_ref)))
+    ]
+    for c in fetch:
+        c.start()
     fac = Factors(factors_ref, nb, heads)
     wanted = [[b * heads + h for h in range(heads)] for b in range(nb)]
     for name, ref in (("growth", growth_ref), ("beyond", beyond_ref)):
         for b, a in enumerate(spread(fac.all(name), wanted, heads * e)):
             ref[b * BLK : (b + 1) * BLK, :] = a
+    fetch[0].wait()
     for b in range(nb):
         causal, decays = fac.decays(b)
         for h in range(heads):
-            scores = mm(block(q_ref, b, h, e), block(k_ref, b, h, e), NT)
+            q = block(q_ref, b, h, e)
+            scores = mm(q, block(k_ref, b, h, e), NT)
             weights = jnp.where(causal, scores * decays[h], 0.0).astype(BF16)
             w_ref[b, h] = weights
             within_ref[b * BLK : (b + 1) * BLK, h * e : (h + 1) * e] = mm(
                 weights, block(v_ref, b, h, e)
             )
+            lifted_ref[b, h] = (q.T.astype(F32) * fac.row("growth", b, h)).astype(BF16)
+    fetch[1].wait()
 
 
 def row_sums(a):
@@ -232,7 +245,7 @@
     sums_ref[...] = jnp.concatenate(parts, axis=0)
 
 
-def grad_kernel(dims, full_width, parts, factors_ref, q_ref, cot_ref, att_ref, *refs):
+def grad_kernel(dims, full_width, parts, factors_ref, lifted_ref, cot_ref, att_ref, *refs):
     sums_refs, (g_ref, scale_ref, payload_ref, local_ref) = refs[:parts], refs[parts:]
     nb, heads, e = dims
     fac = Factors(factors_ref, nb, heads)
@@ -252,8 +265,7 @@
     for h in range(heads):
         running = None
         for b in reversed(range(nb)):
-            lifted = (block(q_ref, b, h, e).T.astype(F32) * fac.row("growth", b, h)).astype(BF16)
-            term = mm(lifted, block(g_ref, b, h, e))
+            term = mm(lifted_ref[b, h], block(g_ref, b, h, e))
             running = term if running is None else fac.row("decay", b, h, e) * running + term
             if b:
                 local_ref[b - 1, h] = running
@@ -324,18 +336,19 @@
         c.wait()
 
 
-def call(kernel, name, args, outs, flops, hbm_in=False, hbm_outs=0, scratch=()):
+def call(kernel, name, args, outs, flops, hbm_ins=0, hbm_outs=0, scratch=()):
     traffic = sum(a.size * a.dtype.itemsize for a in args) + sum(
         math.prod(s) * jnp.dtype(d).itemsize for s, d in outs
     )
     hbm = pl.BlockSpec(memory_space=pltpu.HBM)
-    vmem, smem = pl.BlockSpec(memory_space=pltpu.VMEM), pl.BlockSpec(memory_space=pltpu.SMEM)
-    if hbm_in:
-        args = [pltpu.with_memory_space_constraint(a, pltpu.HBM) for a in args]
+    vmem = pl.BlockSpec(memory_space=pltpu.VMEM)
+    args = [
+        pltpu.with_memory_space_constraint(a, pltpu.HBM) if i < hbm_ins else a for i, a in enumerate(args)
+    ]
     return pl.pallas_call(
         kernel,
         out_shape=[(pltpu.HBM if i < hbm_outs else pltpu.VMEM)(s, d) for i, (s, d) in enumerate(outs)],
-        in_specs=[hbm if hbm_in else smem if a.ndim == 1 else vmem for a in args],
+        in_specs=[hbm if i < hbm_ins else vmem for i in range(len(args))],
         out_specs=[hbm if i < hbm_outs else vmem for i in range(len(outs))],
         scratch_shapes=scratch,
         compiler_params=pltpu.CompilerParams(vmem_limit_bytes=16 * 2**20),
@@ -381,12 +394,11 @@
 
 def sum_over_heads(sums):
     size = lax.axis_size("head")
-    parts, bit, width = [sums], 1, 2
-    while bit < size:
+    rounds = [range(1, min(4, size))] + [[bit] for bit in (4, 8, 16, 32, 64, 128) if bit < size]
+    parts = [sums]
+    for apart in rounds:
         own = functools.reduce(jnp.add, parts)
-        width = min(width, size // bit)
-        parts = [own] + [swap(own, "head", bit * i) for i in range(1, width)]
-        bit, width = bit * width, 4
+        parts = [own] + [swap(own, "head", k) for k in apart]
     return parts
 
 
@@ -405,16 +417,15 @@
     big = 2 * tokens * heads * e * BLK
     small = 2 * tokens * heads * e * e
 
-    state, prefix, factors, q, k, v, cot = call(
-        functools.partial(states_kernel, dims), "states",
-        (decay_code, bnd, queries, keys, values, cotangent),
-        (payload, local, ((len(ROWS) * up8(nb * heads), BLK), F32), narrow, narrow, narrow, narrow), small,
-        hbm_in=True,
-        scratch=(pltpu.SMEM((heads,), jnp.int32), pltpu.VMEM(bnd.shape, jnp.int32), pltpu.SemaphoreType.DMA((6,))),
-    )
-    masks, states, (weights, within, growth, beyond) = gather_states(state, lambda: call(
-        functools.partial(within_kernel, dims), "within", (factors, q, k, v),
-        (((nb, heads, BLK, BLK), BF16), wide, wide, wide), 2 * big,
+    state, prefix, factors, k, v = call(
+        functools.partial(states_kernel, dims), "states", (decay_code, bnd, keys, values),
+        (payload, local, ((len(ROWS) * up8(nb * heads), BLK), F32), narrow, narrow), small, hbm_ins=4,
+        scratch=(pltpu.SMEM((heads,), jnp.int32), pltpu.VMEM(bnd.shape, jnp.int32), pltpu.SemaphoreType.DMA((4,))),
+    )
+    masks, states, (weights, within, growth, beyond, lifted, q, cot) = gather_states(state, lambda: call(
+        functools.partial(within_kernel, dims), "within", (queries, cotangent, factors, k, v),
+        (((nb, heads, BLK, BLK), BF16), wide, wide, wide, ((nb, heads, e, BLK), BF16), narrow, narrow), 2 * big,
+        hbm_ins=2, scratch=(pltpu.SemaphoreType.DMA((2,)),),
     ))
     held, attended, sums = call(
         functools.partial(attend_kernel, dims, masks), "attend",
@@ -424,7 +435,7 @@
     sums = sum_over_heads(sums)
     grad, scale, grad_state, suffix = call(
         functools.partial(grad_kernel, dims, full_width, len(sums)), "grad",
-        (factors, q, cot, attended, *sums),
+        (factors, lifted, cot, attended, *sums),
         (narrow, ((up8(2 * nb), BLK), F32), payload, local), small,
     )
     masks, grad_states, (output, grad_queries, gk_part, gv_part) = gather_states(grad_state, lambda: call(

time: 31.3 us -> 30.6 us (0.978)
  waiting for transfers between devices: 11.6 us -> 9.84 us
  Pallas kernels: 8.02 us -> 9.12 us
    ppermute x10, waiting for transfers between devices: 11.6 us -> 9.84 us  [swap(): lax.ppermute(a, axis, [(i, i ^ mask) for i in range(lax.axis_size(axis))])]
    pallas_call x6, Pallas kernels: 8.02 us -> 9.12 us  [call(): pl.pallas_call(kernel, out_shape=[(pltpu.HBM if i < hbm_outs else pltpu.V...]
  transfers between devices with their start and end apart: 10 -> 10, of which waited for: 7 -> 8; matrix products, arithmetic and copies ran while one was open for 0% -> 0% of each run, Pallas kernels for 13% -> 17%
where the time goes in v3:
time: 30.6 us; the launch traced here: 30.4 us
  starting transfers between devices  10.8 us (35%)
  waiting for transfers between devices  9.84 us (32%)
  Pallas kernels  9.12 us (30%)
  between operations  0.68 us (2%)
    ppermute x10, starting transfers between devices, swap(): lax.ppermute(a, axis, [(i, i ^ mask) for i in range(lax.axis_size(axis))])  10.8 us
    ppermute x10, waiting for transfers between devices, swap(): lax.ppermute(a, axis, [(i, i ^ mask) for i in range(lax.axis_size(axis))])  9.84 us
    pallas_call x6, Pallas kernels, call(): pl.pallas_call(kernel, out_shape=[(pltpu.HBM if i < hbm_outs else pltpu.V...  9.12 us
  transfers between devices with their start and end apart: 10, of which 8 were waited for; matrix products, arithmetic and copies ran while one was open for 0% of the time, Pallas kernels for 17%

profile of v3, /device:TPU:0, one launch (start us, length us, event | category | flops | bytes accessed | tf_op | source)
XLA Modules:
  0.0 30.4 jit_solution(14181489151370444514)
XLA Ops:
  0.6 1.5 %states.1 = (f32[264,128]{1,0:T(8,128)S(1)}, f32[2,2,128,128]{3,2,1,0:T(8,128)S(1)}, f32[48,256]{1,0:T(8,128)S(1)}, bf16[768,256]{1,0:T(8,128)(2,1)S(1)}, bf16[768,256]{1,0:T(8,128)(2,1)S(1)}) custom-call(s32[2]{0:T(128)} %code_in.1, s32[6,128]{1,0:T(8,128)} %bitcast.1, bf16[768,256]{1,0:T(8,128)(2,1)} %k_in.1, bf16[768,256]{1,0:T(8,128)(2,1)} %v_in.1), custom_call_target="tpu_custom_call" | custom-call | flops 50331648 | bytes 2022408 | tf_op jit(solution)/shard_map/states/pallas_call | solution.py:348
  2.1 3.0 %collective-permute-start = (f32[264,128]{1,0:T(8,128)S(1)}, f32[264,128]{1,0:T(8,128)S(1)}, u32[]{:S(2)}, u32[]{:S(2)}) collective-permute-start(f32[264,128]{1,0:T(8,128)S(1)} %get-tuple-element.38.refs_0_), channel_id=1, source_target_pairs={{0,16},{8,24},{16,0},{24,8},{1,17},{9,25},{17,1},{25,9},{2,18},{10... | collective-permute-start | bytes 405512 | tf_op jit(solution)/shard_map/ppermute | solution.py:378
  5.2 2.4 %within.1 = (bf16[3,2,256,256]{3,2,1,0:T(8,128)(2,1)S(1)}, f32[768,256]{1,0:T(8,128)S(1)}, f32[768,256]{1,0:T(8,128)S(1)}, f32[768,256]{1,0:T(8,128)S(1)}, bf16[...) custom-call(bf16[768,256]{1,0:T(8,128)(2,1)} %q_in.1, ...), custom_call_target="tpu_custom_call" | custom-call | flops 201326592 | bytes 5947392 | tf_op jit(solution)/shard_map/within/pallas_call | solution.py:348
  7.5 1.2 %collective-permute-done.refs_0_ = f32[264,128]{1,0:T(8,128)S(1)} collective-permute-done((f32[264,128]{1,0:T(8,128)S(1)}, f32[264,128]{1,0:T(8,128)S(1)}, u32[]{:S(2)}, u32[]{:S(2)}) %collective-permute-start) | collective-permute-done | bytes 135200 | tf_op jit(solution)/shard_map/ppermute | solution.py:378
  8.7 0.0 collective-permute-start.2
  8.7 0.0 collective-permute-done.1.refs_2_
  8.7 1.3 %collective-permute-done.2.refs_3_ = f32[264,128]{1,0:T(8,128)S(1)} collective-permute-done((f32[264,128]{1,0:T(8,128)S(1)}, f32[264,128]{1,0:T(8,128)S(1)}, u32[]{:S(2)}, u32[]{:S(2)}) %collective-permute-start.2) | collective-permute-done | bytes 135200 | tf_op jit(solution)/shard_map/ppermute | solution.py:378
  10.1 0.5 %attend.1 = (bf16[3,2,128,128]{3,2,1,0:T(8,128)(2,1)S(1)}, f32[768,256]{1,0:T(8,128)S(1)}, f32[8,256]{1,0:T(8,128)S(1)}) custom-call(f32[48,256]{1,0:T(8,128)S(1)} %get-tuple-element.29.factors_ref, bf16[768,256]{1,0:T(8,128)(2,1)S(1)} %get-tuple-element.32.q_ref, bf16[768,256]{1,0:T(8,128)(2,1)S(1)} %get-tuple-element.34.refs_1_.cot_ref, ...), custom_call_target="tpu_custom_call" | custom-call | flops 50331648 | bytes 4202496 | tf_op jit(solution)/shard_map/attend/pallas_call | solution.py:348
  10.6 2.8 %collective-permute-start.5 = (f32[8,256]{1,0:T(8,128)S(1)}, f32[8,256]{1,0:T(8,128)S(1)}, u32[]{:S(2)}, u32[]{:S(2)}) collective-permute-start(f32[8,256]{1,0:T(8,128)S(1)} %get-tuple-element.40), channel_id=1, source_target_pairs={{0,3},{1,2},{2,1},{3,0},{4,7},{5,6},{6,5},{7,4},{8,11},{9,10},{10,... | collective-permute-start | bytes 24584 | tf_op jit(solution)/shard_map/ppermute | solution.py:378
  13.4 0.4 %collective-permute-start.4 = (f32[8,256]{1,0:T(8,128)S(1)}, f32[8,256]{1,0:T(8,128)S(1)}, u32[]{:S(2)}, u32[]{:S(2)}) collective-permute-start(f32[8,256]{1,0:T(8,128)S(1)} %get-tuple-element.40), channel_id=1, source_target_pairs={{0,2},{1,3},{2,0},{3,1},{4,6},{5,7},{6,4},{7,5},{8,10},{9,11},{10,... | collective-permute-start | bytes 24584 | tf_op jit(solution)/shard_map/ppermute | solution.py:378
  13.9 0.3 %collective-permute-start.3 = (f32[8,256]{1,0:T(8,128)S(1)}, f32[8,256]{1,0:T(8,128)S(1)}, u32[]{:S(2)}, u32[]{:S(2)}) collective-permute-start(f32[8,256]{1,0:T(8,128)S(1)} %get-tuple-element.40), channel_id=1, source_target_pairs={{0,1},{1,0},{2,3},{3,2},{4,5},{5,4},{6,7},{7,6},{8,9},{9,8},{10,11... | collective-permute-start | bytes 24584 | tf_op jit(solution)/shard_map/ppermute | solution.py:378
  14.2 1.1 %collective-permute-done.5 = f32[8,256]{1,0:T(8,128)S(1)} collective-permute-done((f32[8,256]{1,0:T(8,128)S(1)}, f32[8,256]{1,0:T(8,128)S(1)}, u32[]{:S(2)}, u32[]{:S(2)}) %collective-permute-start.5) | collective-permute-done | bytes 8224 | tf_op jit(solution)/shard_map/ppermute | solution.py:378
  15.2 1.8 %collective-permute-done.4 = f32[8,256]{1,0:T(8,128)S(1)} collective-permute-done((f32[8,256]{1,0:T(8,128)S(1)}, f32[8,256]{1,0:T(8,128)S(1)}, u32[]{:S(2)}, u32[]{:S(2)}) %collective-permute-start.4) | collective-permute-done | bytes 8224 | tf_op jit(solution)/shard_map/ppermute | solution.py:378
  17.1 0.4 %collective-permute-done.3 = f32[8,256]{1,0:T(8,128)S(1)} collective-permute-done((f32[8,256]{1,0:T(8,128)S(1)}, f32[8,256]{1,0:T(8,128)S(1)}, u32[]{:S(2)}, u32[]{:S(2)}) %collective-permute-start.3) | collective-permute-done | bytes 8224 | tf_op jit(solution)/shard_map/ppermute | solution.py:378
  17.5 2.6 %collective-permute-start.6 = (f32[8,256]{1,0:T(8,128)S(1)}, f32[8,256]{1,0:T(8,128)S(1)}, u32[]{:S(2)}, u32[]{:S(2)}) collective-permute-start(f32[8,256]{1,0:T(8,128)S(1)} %add_add_fusion.refs_0_), channel_id=1, source_target_pairs={{0,4},{1,5},{2,6},{3,7},{4,0},{5,1},{6,2},{7,3},{8,12},{9,13},{10,... | collective-permute-start | bytes 24584 | tf_op jit(solution)/shard_map/ppermute | solution.py:378
  20.1 2.0 %collective-permute-done.6.refs_1_ = f32[8,256]{1,0:T(8,128)S(1)} collective-permute-done((f32[8,256]{1,0:T(8,128)S(1)}, f32[8,256]{1,0:T(8,128)S(1)}, u32[]{:S(2)}, u32[]{:S(2)}) %collective-permute-start.6) | collective-permute-done | bytes 8224 | tf_op jit(solution)/shard_map/ppermute | solution.py:378
  22.1 0.7 %grad.1 = (bf16[768,256]{1,0:T(8,128)(2,1)S(1)}, f32[8,256]{1,0:T(8,128)S(1)}, f32[264,128]{1,0:T(8,128)S(1)}, f32[2,2,128,128]{3,2,1,0:T(8,128)S(1)}) custom-call(f32[48,256]{1,0:T(8,128)S(1)} %get-tuple-element.29.factors_ref, bf16[3,2,128,256]{3,2,1,0:T(8,128)(2,1)S(1)} %get-tuple-element.33.lifted_ref, ...), custom_call_target="tpu_custom_call" | custom-call | flops 50331648 | bytes 2437120 | tf_op jit(solution)/shard_map/grad/pallas_call | solution.py:348
  22.8 1.6 %collective-permute-start.7 = (f32[264,128]{1,0:T(8,128)S(1)}, f32[264,128]{1,0:T(8,128)S(1)}, u32[]{:S(2)}, u32[]{:S(2)}) collective-permute-start(f32[264,128]{1,0:T(8,128)S(1)} %get-tuple-element.51.refs_0_), channel_id=1, source_target_pairs={{0,16},{8,24},{16,0},{24,8},{1,17},{9,25},{17,1},{25,9},{2,18},{10... | collective-permute-start | bytes 405512 | tf_op jit(solution)/shard_map/ppermute | solution.py:378
  24.4 2.8 %inner_grads.1 = (bf16[768,256]{1,0:T(8,128)(2,1)}, bf16[768,256]{1,0:T(8,128)(2,1)}, f32[768,256]{1,0:T(8,128)S(1)}, f32[768,256]{1,0:T(8,128)S(1)}) custom-call(f32[48,256]{1,0:T(8,128)S(1)} %get-tuple-element.29.factors_ref, bf16[768,256]{1,0:T(8,128)(2,1)S(1)} %get-tuple-element.32.q_ref, bf16[768,256]{1,0:T(8,128)(2,1)S(1)} %get-tuple-element.30.k_ref, ...), custom_call_target="tpu_custom_call" | custom-call | flops 452984832 | bytes 6545408 | tf_op jit(solution)/shard_map/inner_grads/pallas_call | solution.py:348
  27.2 0.6 %collective-permute-done.7.refs_0_ = f32[264,128]{1,0:T(8,128)S(1)} collective-permute-done((f32[264,128]{1,0:T(8,128)S(1)}, f32[264,128]{1,0:T(8,128)S(1)}, u32[]{:S(2)}, u32[]{:S(2)}) %collective-permute-start.7) | collective-permute-done | bytes 135200 | tf_op jit(solution)/shard_map/ppermute | solution.py:378
  27.9 0.0 collective-permute-start.9
  27.9 0.0 collective-permute-done.8.refs_2_
  27.9 1.3 %collective-permute-done.9.refs_3_ = f32[264,128]{1,0:T(8,128)S(1)} collective-permute-done((f32[264,128]{1,0:T(8,128)S(1)}, f32[264,128]{1,0:T(8,128)S(1)}, u32[]{:S(2)}, u32[]{:S(2)}) %collective-permute-start.9) | collective-permute-done | bytes 135200 | tf_op jit(solution)/shard_map/ppermute | solution.py:378
  29.2 1.2 %outer_grads.1 = (bf16[768,256]{1,0:T(8,128)(2,1)}, bf16[768,256]{1,0:T(8,128)(2,1)}) custom-call(f32[48,256]{1,0:T(8,128)S(1)} %get-tuple-element.29.factors_ref, bf16[768,256]{1,0:T(8,128)(2,1)S(1)} %get-tuple-element.30.k_ref, bf16[768,256]{1,0:T(8,128)(2,1)S(1)} %get-tuple-element.31.v_ref, f32[768,256]{1,0:T(8,128)S(1)} %get-tuple-element.47.gk_part_ref, ...), custom_call_target="tpu_custom_call" | custom-call | flops 100663296 | bytes 4784128 | tf_op jit(solution)/shard_map/outer_grads/pallas_call | solution.py:348
  (5 shorter events, 0.0 us)
Async XLA Ops:
  2.1 6.6 %collective-permute-start = (f32[264,128]{1,0:T(8,128)S(1)}, f32[264,128]{1,0:T(8,128)S(1)}, u32[]{:S(2)}, u32[]{:S(2)}) collective-permute-start(f32[264,128]{1,0:T(8,128)S(1)} %get-tuple-element.38.refs_0_), channel_id=1, source_target_pairs={{0,16},{8,24},{16,0},{24,8},{1,17},{9,25},{17,1},{25,9},{2,18},{10... | collective-permute-start | bytes 405512 | tf_op jit(solution)/shard_map/ppermute | solution.py:378
  5.2 3.6 %collective-permute-start.1 = (f32[264,128]{1,0:T(8,128)S(1)}, f32[264,128]{1,0:T(8,128)S(1)}, u32[]{:S(2)}, u32[]{:S(2)}) collective-permute-start(f32[264,128]{1,0:T(8,128)S(1)} %get-tuple-element.38.refs_0_), channel_id=1, source_target_pairs={{0,8},{8,0},{16,24},{24,16},{1,9},{9,1},{17,25},{25,17},{2,10},{10... | collective-permute-start | bytes 405512 | tf_op jit(solution)/shard_map/ppermute | solution.py:378
  8.7 1.4 %collective-permute-start.2 = (f32[264,128]{1,0:T(8,128)S(1)}, f32[264,128]{1,0:T(8,128)S(1)}, u32[]{:S(2)}, u32[]{:S(2)}) collective-permute-start(f32[264,128]{1,0:T(8,128)S(1)} %after.2.refs_1_), channel_id=1, source_target_pairs={{0,8},{8,0},{16,24},{24,16},{1,9},{9,1},{17,25},{25,17},{2,10},{10... | collective-permute-start | bytes 405512 | tf_op jit(solution)/shard_map/ppermute | solution.py:378
  10.6 4.6 %collective-permute-start.5 = (f32[8,256]{1,0:T(8,128)S(1)}, f32[8,256]{1,0:T(8,128)S(1)}, u32[]{:S(2)}, u32[]{:S(2)}) collective-permute-start(f32[8,256]{1,0:T(8,128)S(1)} %get-tuple-element.40), channel_id=1, source_target_pairs={{0,3},{1,2},{2,1},{3,0},{4,7},{5,6},{6,5},{7,4},{8,11},{9,10},{10,... | collective-permute-start | bytes 24584 | tf_op jit(solution)/shard_map/ppermute | solution.py:378
  13.4 3.7 %collective-permute-start.4 = (f32[8,256]{1,0:T(8,128)S(1)}, f32[8,256]{1,0:T(8,128)S(1)}, u32[]{:S(2)}, u32[]{:S(2)}) collective-permute-start(f32[8,256]{1,0:T(8,128)S(1)} %get-tuple-element.40), channel_id=1, source_target_pairs={{0,2},{1,3},{2,0},{3,1},{4,6},{5,7},{6,4},{7,5},{8,10},{9,11},{10,... | collective-permute-start | bytes 24584 | tf_op jit(solution)/shard_map/ppermute | solution.py:378
  13.9 3.7 %collective-permute-start.3 = (f32[8,256]{1,0:T(8,128)S(1)}, f32[8,256]{1,0:T(8,128)S(1)}, u32[]{:S(2)}, u32[]{:S(2)}) collective-permute-start(f32[8,256]{1,0:T(8,128)S(1)} %get-tuple-element.40), channel_id=1, source_target_pairs={{0,1},{1,0},{2,3},{3,2},{4,5},{5,4},{6,7},{7,6},{8,9},{9,8},{10,11... | collective-permute-start | bytes 24584 | tf_op jit(solution)/shard_map/ppermute | solution.py:378
  17.5 4.5 %collective-permute-start.6 = (f32[8,256]{1,0:T(8,128)S(1)}, f32[8,256]{1,0:T(8,128)S(1)}, u32[]{:S(2)}, u32[]{:S(2)}) collective-permute-start(f32[8,256]{1,0:T(8,128)S(1)} %add_add_fusion.refs_0_), channel_id=1, source_target_pairs={{0,4},{1,5},{2,6},{3,7},{4,0},{5,1},{6,2},{7,3},{8,12},{9,13},{10,... | collective-permute-start | bytes 24584 | tf_op jit(solution)/shard_map/ppermute | solution.py:378
  22.8 5.1 %collective-permute-start.7 = (f32[264,128]{1,0:T(8,128)S(1)}, f32[264,128]{1,0:T(8,128)S(1)}, u32[]{:S(2)}, u32[]{:S(2)}) collective-permute-start(f32[264,128]{1,0:T(8,128)S(1)} %get-tuple-element.51.refs_0_), channel_id=1, source_target_pairs={{0,16},{8,24},{16,0},{24,8},{1,17},{9,25},{17,1},{25,9},{2,18},{10... | collective-permute-start | bytes 405512 | tf_op jit(solution)/shard_map/ppermute | solution.py:378
  24.4 3.5 %collective-permute-start.8 = (f32[264,128]{1,0:T(8,128)S(1)}, f32[264,128]{1,0:T(8,128)S(1)}, u32[]{:S(2)}, u32[]{:S(2)}) collective-permute-start(f32[264,128]{1,0:T(8,128)S(1)} %get-tuple-element.51.refs_0_), channel_id=1, source_target_pairs={{0,8},{8,0},{16,24},{24,16},{1,9},{9,1},{17,25},{25,17},{2,10},{10... | collective-permute-start | bytes 405512 | tf_op jit(solution)/shard_map/ppermute | solution.py:378
  27.9 1.4 %collective-permute-start.9 = (f32[264,128]{1,0:T(8,128)S(1)}, f32[264,128]{1,0:T(8,128)S(1)}, u32[]{:S(2)}, u32[]{:S(2)}) collective-permute-start(f32[264,128]{1,0:T(8,128)S(1)} %after.3.refs_1_), channel_id=1, source_target_pairs={{0,8},{8,0},{16,24},{24,16},{1,9},{9,1},{17,25},{25,17},{2,10},{10... | collective-permute-start | bytes 405512 | tf_op jit(solution)/shard_map/ppermute | solution.py:378

commit v4 on v3

--- a/solution.py
+++ b/solution.py
@@ -256,20 +256,21 @@
     squared = scale * scale
     lean = jnp.concatenate([squared[:nb], squared[:nb], squared[2 * nb :]], axis=0) * sums / full_width
     factors = jnp.where(iota(sums.shape, 0) < nb, scale, lean)
-    columns = spread(factors, [[r] for r in range(2 * nb)], heads * e)
-    for b in range(nb):
+    columns = spread(factors, [[r] for r in range(2 * nb)], e)
+    running = [None] * heads
+    for b in reversed(range(nb)):
         rows = slice(b * BLK, (b + 1) * BLK)
-        g_ref[rows, :] = (
-            columns[b] * (cot_ref[rows, :].astype(F32) - att_ref[rows, :] * columns[nb + b])
-        ).astype(BF16)
+        for h in range(heads):
+            cols = slice(h * e, (h + 1) * e)
+            g = columns[b] * (cot_ref[rows, cols].astype(F32) - att_ref[rows, cols] * columns[nb + b])
+            g = g.astype(BF16)
+            g_ref[rows, cols] = g
+            term = mm(lifted_ref[b, h], g)
+            running[h] = term if b == nb - 1 else fac.row("decay", b, h, e) * running[h] + term
+            if b:
+                local_ref[b - 1, h] = running[h]
     for h in range(heads):
-        running = None
-        for b in reversed(range(nb)):
-            term = mm(lifted_ref[b, h], block(g_ref, b, h, e))
-            running = term if running is None else fac.row("decay", b, h, e) * running + term
-            if b:
-                local_ref[b - 1, h] = running
-        payload_ref[h * e : (h + 1) * e, :] = running
+        payload_ref[h * e : (h + 1) * e, :] = running[h]
     store_totals(payload_ref, fac, e)
 
 

time: 30.6 us -> 30.5 us (level)
  no operation moved by 1% of the time
where the time goes in v4:
time: 30.5 us; the launch traced here: 30.4 us
  starting transfers between devices  10.8 us (35%)
  waiting for transfers between devices  9.83 us (32%)
  Pallas kernels  9.08 us (30%)
  between operations  0.68 us (2%)
    ppermute x10, starting transfers between devices, swap(): lax.ppermute(a, axis, [(i, i ^ mask) for i in range(lax.axis_size(axis))])  10.8 us
    ppermute x10, waiting for transfers between devices, swap(): lax.ppermute(a, axis, [(i, i ^ mask) for i in range(lax.axis_size(axis))])  9.83 us
    pallas_call x6, Pallas kernels, call(): pl.pallas_call(kernel, out_shape=[(pltpu.HBM if i < hbm_outs else pltpu.V...  9.08 us
  transfers between devices with their start and end apart: 10, of which 8 were waited for; matrix products, arithmetic and copies ran while one was open for 0% of the time, Pallas kernels for 17%

profile of v4, /device:TPU:0, one launch (start us, length us, event | category | flops | bytes accessed | tf_op | source)
XLA Modules:
  0.0 30.4 jit_solution(5979511605461847020)
XLA Ops:
  0.6 1.5 %states.1 = (f32[264,128]{1,0:T(8,128)S(1)}, f32[2,2,128,128]{3,2,1,0:T(8,128)S(1)}, f32[48,256]{1,0:T(8,128)S(1)}, bf16[768,256]{1,0:T(8,128)(2,1)S(1)}, bf16[768,256]{1,0:T(8,128)(2,1)S(1)}) custom-call(s32[2]{0:T(128)} %code_in.1, s32[6,128]{1,0:T(8,128)} %bitcast.1, bf16[768,256]{1,0:T(8,128)(2,1)} %k_in.1, bf16[768,256]{1,0:T(8,128)(2,1)} %v_in.1), custom_call_target="tpu_custom_call" | custom-call | flops 50331648 | bytes 2022408 | tf_op jit(solution)/shard_map/states/pallas_call | solution.py:349
  2.1 3.0 %collective-permute-start = (f32[264,128]{1,0:T(8,128)S(1)}, f32[264,128]{1,0:T(8,128)S(1)}, u32[]{:S(2)}, u32[]{:S(2)}) collective-permute-start(f32[264,128]{1,0:T(8,128)S(1)} %get-tuple-element.38.refs_0_), channel_id=1, source_target_pairs={{0,16},{8,24},{16,0},{24,8},{1,17},{9,25},{17,1},{25,9},{2,18},{10... | collective-permute-start | bytes 405512 | tf_op jit(solution)/shard_map/ppermute | solution.py:379
  5.2 0.0 collective-permute-start.1
  5.2 2.4 %within.1 = (bf16[3,2,256,256]{3,2,1,0:T(8,128)(2,1)S(1)}, f32[768,256]{1,0:T(8,128)S(1)}, f32[768,256]{1,0:T(8,128)S(1)}, f32[768,256]{1,0:T(8,128)S(1)}, bf16[...) custom-call(bf16[768,256]{1,0:T(8,128)(2,1)} %q_in.1, ...), custom_call_target="tpu_custom_call" | custom-call | flops 201326592 | bytes 5947392 | tf_op jit(solution)/shard_map/within/pallas_call | solution.py:349
  7.5 1.2 %collective-permute-done.refs_0_ = f32[264,128]{1,0:T(8,128)S(1)} collective-permute-done((f32[264,128]{1,0:T(8,128)S(1)}, f32[264,128]{1,0:T(8,128)S(1)}, u32[]{:S(2)}, u32[]{:S(2)}) %collective-permute-start) | collective-permute-done | bytes 135200 | tf_op jit(solution)/shard_map/ppermute | solution.py:379
  8.7 0.0 collective-permute-start.2
  8.7 0.0 collective-permute-done.1.refs_2_
  8.7 1.3 %collective-permute-done.2.refs_3_ = f32[264,128]{1,0:T(8,128)S(1)} collective-permute-done((f32[264,128]{1,0:T(8,128)S(1)}, f32[264,128]{1,0:T(8,128)S(1)}, u32[]{:S(2)}, u32[]{:S(2)}) %collective-permute-start.2) | collective-permute-done | bytes 135200 | tf_op jit(solution)/shard_map/ppermute | solution.py:379
  10.1 0.5 %attend.1 = (bf16[3,2,128,128]{3,2,1,0:T(8,128)(2,1)S(1)}, f32[768,256]{1,0:T(8,128)S(1)}, f32[8,256]{1,0:T(8,128)S(1)}) custom-call(f32[48,256]{1,0:T(8,128)S(1)} %get-tuple-element.29.factors_ref, bf16[768,256]{1,0:T(8,128)(2,1)S(1)} %get-tuple-element.32.q_ref, bf16[768,256]{1,0:T(8,128)(2,1)S(1)} %get-tuple-element.34.refs_1_.cot_ref, ...), custom_call_target="tpu_custom_call" | custom-call | flops 50331648 | bytes 4202496 | tf_op jit(solution)/shard_map/attend/pallas_call | solution.py:349
  10.6 2.8 %collective-permute-start.5 = (f32[8,256]{1,0:T(8,128)S(1)}, f32[8,256]{1,0:T(8,128)S(1)}, u32[]{:S(2)}, u32[]{:S(2)}) collective-permute-start(f32[8,256]{1,0:T(8,128)S(1)} %get-tuple-element.40), channel_id=1, source_target_pairs={{0,3},{1,2},{2,1},{3,0},{4,7},{5,6},{6,5},{7,4},{8,11},{9,10},{10,... | collective-permute-start | bytes 24584 | tf_op jit(solution)/shard_map/ppermute | solution.py:379
  13.4 0.4 %collective-permute-start.4 = (f32[8,256]{1,0:T(8,128)S(1)}, f32[8,256]{1,0:T(8,128)S(1)}, u32[]{:S(2)}, u32[]{:S(2)}) collective-permute-start(f32[8,256]{1,0:T(8,128)S(1)} %get-tuple-element.40), channel_id=1, source_target_pairs={{0,2},{1,3},{2,0},{3,1},{4,6},{5,7},{6,4},{7,5},{8,10},{9,11},{10,... | collective-permute-start | bytes 24584 | tf_op jit(solution)/shard_map/ppermute | solution.py:379
  13.9 0.3 %collective-permute-start.3 = (f32[8,256]{1,0:T(8,128)S(1)}, f32[8,256]{1,0:T(8,128)S(1)}, u32[]{:S(2)}, u32[]{:S(2)}) collective-permute-start(f32[8,256]{1,0:T(8,128)S(1)} %get-tuple-element.40), channel_id=1, source_target_pairs={{0,1},{1,0},{2,3},{3,2},{4,5},{5,4},{6,7},{7,6},{8,9},{9,8},{10,11... | collective-permute-start | bytes 24584 | tf_op jit(solution)/shard_map/ppermute | solution.py:379
  14.2 1.1 %collective-permute-done.5 = f32[8,256]{1,0:T(8,128)S(1)} collective-permute-done((f32[8,256]{1,0:T(8,128)S(1)}, f32[8,256]{1,0:T(8,128)S(1)}, u32[]{:S(2)}, u32[]{:S(2)}) %collective-permute-start.5) | collective-permute-done | bytes 8224 | tf_op jit(solution)/shard_map/ppermute | solution.py:379
  15.2 1.8 %collective-permute-done.4 = f32[8,256]{1,0:T(8,128)S(1)} collective-permute-done((f32[8,256]{1,0:T(8,128)S(1)}, f32[8,256]{1,0:T(8,128)S(1)}, u32[]{:S(2)}, u32[]{:S(2)}) %collective-permute-start.4) | collective-permute-done | bytes 8224 | tf_op jit(solution)/shard_map/ppermute | solution.py:379
  17.1 0.4 %collective-permute-done.3 = f32[8,256]{1,0:T(8,128)S(1)} collective-permute-done((f32[8,256]{1,0:T(8,128)S(1)}, f32[8,256]{1,0:T(8,128)S(1)}, u32[]{:S(2)}, u32[]{:S(2)}) %collective-permute-start.3) | collective-permute-done | bytes 8224 | tf_op jit(solution)/shard_map/ppermute | solution.py:379
  17.5 2.6 %collective-permute-start.6 = (f32[8,256]{1,0:T(8,128)S(1)}, f32[8,256]{1,0:T(8,128)S(1)}, u32[]{:S(2)}, u32[]{:S(2)}) collective-permute-start(f32[8,256]{1,0:T(8,128)S(1)} %add_add_fusion.refs_0_), channel_id=1, source_target_pairs={{0,4},{1,5},{2,6},{3,7},{4,0},{5,1},{6,2},{7,3},{8,12},{9,13},{10,... | collective-permute-start | bytes 24584 | tf_op jit(solution)/shard_map/ppermute | solution.py:379
  20.1 2.0 %collective-permute-done.6.refs_1_ = f32[8,256]{1,0:T(8,128)S(1)} collective-permute-done((f32[8,256]{1,0:T(8,128)S(1)}, f32[8,256]{1,0:T(8,128)S(1)}, u32[]{:S(2)}, u32[]{:S(2)}) %collective-permute-start.6) | collective-permute-done | bytes 8224 | tf_op jit(solution)/shard_map/ppermute | solution.py:379
  22.1 0.7 %grad.1 = (bf16[768,256]{1,0:T(8,128)(2,1)S(1)}, f32[8,256]{1,0:T(8,128)S(1)}, f32[264,128]{1,0:T(8,128)S(1)}, f32[2,2,128,128]{3,2,1,0:T(8,128)S(1)}) custom-call(f32[48,256]{1,0:T(8,128)S(1)} %get-tuple-element.29.factors_ref, bf16[3,2,128,256]{3,2,1,0:T(8,128)(2,1)S(1)} %get-tuple-element.33.lifted_ref, ...), custom_call_target="tpu_custom_call" | custom-call | flops 50331648 | bytes 2437120 | tf_op jit(solution)/shard_map/grad/pallas_call | solution.py:349
  22.7 1.6 %collective-permute-start.7 = (f32[264,128]{1,0:T(8,128)S(1)}, f32[264,128]{1,0:T(8,128)S(1)}, u32[]{:S(2)}, u32[]{:S(2)}) collective-permute-start(f32[264,128]{1,0:T(8,128)S(1)} %get-tuple-element.51.refs_0_), channel_id=1, source_target_pairs={{0,16},{8,24},{16,0},{24,8},{1,17},{9,25},{17,1},{25,9},{2,18},{10... | collective-permute-start | bytes 405512 | tf_op jit(solution)/shard_map/ppermute | solution.py:379
  24.3 0.0 collective-permute-start.8
  24.3 2.8 %inner_grads.1 = (bf16[768,256]{1,0:T(8,128)(2,1)}, bf16[768,256]{1,0:T(8,128)(2,1)}, f32[768,256]{1,0:T(8,128)S(1)}, f32[768,256]{1,0:T(8,128)S(1)}) custom-call(f32[48,256]{1,0:T(8,128)S(1)} %get-tuple-element.29.factors_ref, bf16[768,256]{1,0:T(8,128)(2,1)S(1)} %get-tuple-element.32.q_ref, bf16[768,256]{1,0:T(8,128)(2,1)S(1)} %get-tuple-element.30.k_ref, ...), custom_call_target="tpu_custom_call" | custom-call | flops 452984832 | bytes 6545408 | tf_op jit(solution)/shard_map/inner_grads/pallas_call | solution.py:349
  27.2 0.6 %collective-permute-done.7.refs_0_ = f32[264,128]{1,0:T(8,128)S(1)} collective-permute-done((f32[264,128]{1,0:T(8,128)S(1)}, f32[264,128]{1,0:T(8,128)S(1)}, u32[]{:S(2)}, u32[]{:S(2)}) %collective-permute-start.7) | collective-permute-done | bytes 135200 | tf_op jit(solution)/shard_map/ppermute | solution.py:379
  27.8 1.3 %collective-permute-done.9.refs_3_ = f32[264,128]{1,0:T(8,128)S(1)} collective-permute-done((f32[264,128]{1,0:T(8,128)S(1)}, f32[264,128]{1,0:T(8,128)S(1)}, u32[]{:S(2)}, u32[]{:S(2)}) %collective-permute-start.9) | collective-permute-done | bytes 135200 | tf_op jit(solution)/shard_map/ppermute | solution.py:379
  29.2 1.2 %outer_grads.1 = (bf16[768,256]{1,0:T(8,128)(2,1)}, bf16[768,256]{1,0:T(8,128)(2,1)}) custom-call(f32[48,256]{1,0:T(8,128)S(1)} %get-tuple-element.29.factors_ref, bf16[768,256]{1,0:T(8,128)(2,1)S(1)} %get-tuple-element.30.k_ref, bf16[768,256]{1,0:T(8,128)(2,1)S(1)} %get-tuple-element.31.v_ref, f32[768,256]{1,0:T(8,128)S(1)} %get-tuple-element.47.gk_part_ref, ...), custom_call_target="tpu_custom_call" | custom-call | flops 100663296 | bytes 4784128 | tf_op jit(solution)/shard_map/outer_grads/pallas_call | solution.py:349
  (5 shorter events, 0.0 us)
Async XLA Ops:
  2.1 6.6 %collective-permute-start = (f32[264,128]{1,0:T(8,128)S(1)}, f32[264,128]{1,0:T(8,128)S(1)}, u32[]{:S(2)}, u32[]{:S(2)}) collective-permute-start(f32[264,128]{1,0:T(8,128)S(1)} %get-tuple-element.38.refs_0_), channel_id=1, source_target_pairs={{0,16},{8,24},{16,0},{24,8},{1,17},{9,25},{17,1},{25,9},{2,18},{10... | collective-permute-start | bytes 405512 | tf_op jit(solution)/shard_map/ppermute | solution.py:379
  5.2 3.6 %collective-permute-start.1 = (f32[264,128]{1,0:T(8,128)S(1)}, f32[264,128]{1,0:T(8,128)S(1)}, u32[]{:S(2)}, u32[]{:S(2)}) collective-permute-start(f32[264,128]{1,0:T(8,128)S(1)} %get-tuple-element.38.refs_0_), channel_id=1, source_target_pairs={{0,8},{8,0},{16,24},{24,16},{1,9},{9,1},{17,25},{25,17},{2,10},{10... | collective-permute-start | bytes 405512 | tf_op jit(solution)/shard_map/ppermute | solution.py:379
  8.7 1.4 %collective-permute-start.2 = (f32[264,128]{1,0:T(8,128)S(1)}, f32[264,128]{1,0:T(8,128)S(1)}, u32[]{:S(2)}, u32[]{:S(2)}) collective-permute-start(f32[264,128]{1,0:T(8,128)S(1)} %after.2.refs_1_), channel_id=1, source_target_pairs={{0,8},{8,0},{16,24},{24,16},{1,9},{9,1},{17,25},{25,17},{2,10},{10... | collective-permute-start | bytes 405512 | tf_op jit(solution)/shard_map/ppermute | solution.py:379
  10.6 4.6 %collective-permute-start.5 = (f32[8,256]{1,0:T(8,128)S(1)}, f32[8,256]{1,0:T(8,128)S(1)}, u32[]{:S(2)}, u32[]{:S(2)}) collective-permute-start(f32[8,256]{1,0:T(8,128)S(1)} %get-tuple-element.40), channel_id=1, source_target_pairs={{0,3},{1,2},{2,1},{3,0},{4,7},{5,6},{6,5},{7,4},{8,11},{9,10},{10,... | collective-permute-start | bytes 24584 | tf_op jit(solution)/shard_map/ppermute | solution.py:379
  13.4 3.7 %collective-permute-start.4 = (f32[8,256]{1,0:T(8,128)S(1)}, f32[8,256]{1,0:T(8,128)S(1)}, u32[]{:S(2)}, u32[]{:S(2)}) collective-permute-start(f32[8,256]{1,0:T(8,128)S(1)} %get-tuple-element.40), channel_id=1, source_target_pairs={{0,2},{1,3},{2,0},{3,1},{4,6},{5,7},{6,4},{7,5},{8,10},{9,11},{10,... | collective-permute-start | bytes 24584 | tf_op jit(solution)/shard_map/ppermute | solution.py:379
  13.9 3.7 %collective-permute-start.3 = (f32[8,256]{1,0:T(8,128)S(1)}, f32[8,256]{1,0:T(8,128)S(1)}, u32[]{:S(2)}, u32[]{:S(2)}) collective-permute-start(f32[8,256]{1,0:T(8,128)S(1)} %get-tuple-element.40), channel_id=1, source_target_pairs={{0,1},{1,0},{2,3},{3,2},{4,5},{5,4},{6,7},{7,6},{8,9},{9,8},{10,11... | collective-permute-start | bytes 24584 | tf_op jit(solution)/shard_map/ppermute | solution.py:379
  17.5 4.5 %collective-permute-start.6 = (f32[8,256]{1,0:T(8,128)S(1)}, f32[8,256]{1,0:T(8,128)S(1)}, u32[]{:S(2)}, u32[]{:S(2)}) collective-permute-start(f32[8,256]{1,0:T(8,128)S(1)} %add_add_fusion.refs_0_), channel_id=1, source_target_pairs={{0,4},{1,5},{2,6},{3,7},{4,0},{5,1},{6,2},{7,3},{8,12},{9,13},{10,... | collective-permute-start | bytes 24584 | tf_op jit(solution)/shard_map/ppermute | solution.py:379
  22.7 5.1 %collective-permute-start.7 = (f32[264,128]{1,0:T(8,128)S(1)}, f32[264,128]{1,0:T(8,128)S(1)}, u32[]{:S(2)}, u32[]{:S(2)}) collective-permute-start(f32[264,128]{1,0:T(8,128)S(1)} %get-tuple-element.51.refs_0_), channel_id=1, source_target_pairs={{0,16},{8,24},{16,0},{24,8},{1,17},{9,25},{17,1},{25,9},{2,18},{10... | collective-permute-start | bytes 405512 | tf_op jit(solution)/shard_map/ppermute | solution.py:379
  24.3 3.5 %collective-permute-start.8 = (f32[264,128]{1,0:T(8,128)S(1)}, f32[264,128]{1,0:T(8,128)S(1)}, u32[]{:S(2)}, u32[]{:S(2)}) collective-permute-start(f32[264,128]{1,0:T(8,128)S(1)} %get-tuple-element.51.refs_0_), channel_id=1, source_target_pairs={{0,8},{8,0},{16,24},{24,16},{1,9},{9,1},{17,25},{25,17},{2,10},{10... | collective-permute-start | bytes 405512 | tf_op jit(solution)/shard_map/ppermute | solution.py:379
  27.8 1.4 %collective-permute-start.9 = (f32[264,128]{1,0:T(8,128)S(1)}, f32[264,128]{1,0:T(8,128)S(1)}, u32[]{:S(2)}, u32[]{:S(2)}) collective-permute-start(f32[264,128]{1,0:T(8,128)S(1)} %after.3.refs_1_), channel_id=1, source_target_pairs={{0,8},{8,0},{16,24},{24,16},{1,9},{9,1},{17,25},{25,17},{2,10},{10... | collective-permute-start | bytes 405512 | tf_op jit(solution)/shard_map/ppermute | solution.py:379

commit v5 on v4

--- a/solution.py
+++ b/solution.py
@@ -318,19 +318,20 @@
     copies = []
     for b in reversed(range(nb)):
         rows = slice(b * BLK, (b + 1) * BLK)
+        held = []
         for h in range(heads):
-            cols = slice(h * e, (h + 1) * e)
             state = jnp.exp(behind[h]) * arrived[h]
             if b < nb - 1:
                 state = state + local_ref[b, h]
             behind[h] = behind[h] + fac.row("total", b, h, e)
-            held = state.astype(BF16)
-            far = beyond_ref[rows, cols]
-            gk = gk_part_ref[rows, cols] + far * mm(block(v_ref, b, h, e), held, NT)
-            gk_ref[rows, cols] = gk.astype(BF16)
-            gv = gv_part_ref[rows, cols] + far * mm(block(k_ref, b, h, e), held)
-            gv_ref[rows, cols] = gv.astype(BF16)
-        for i, (s, d) in enumerate(((gk_ref, gk_hbm), (gv_ref, gv_hbm))):
+            held.append(state.astype(BF16))
+        for i, (of, part, s, d) in enumerate(
+            ((v_ref, gk_part_ref, gk_ref, gk_hbm), (k_ref, gv_part_ref, gv_ref, gv_hbm))
+        ):
+            for h in range(heads):
+                cols = slice(h * e, (h + 1) * e)
+                far = mm(block(of, b, h, e), held[h], NN if i else NT)
+                s[rows, cols] = (part[rows, cols] + beyond_ref[rows, cols] * far).astype(BF16)
             copies.append(pltpu.make_async_copy(s.at[rows], d.at[rows], sems.at[2 * b + i]))
             copies[-1].start()
     for c in copies:

time: 30.5 us -> 30.5 us (level)
  no operation moved by 1% of the time
where the time goes in v5:
time: 30.5 us; the launch traced here: 30.3 us
  starting transfers between devices  10.8 us (35%)
  waiting for transfers between devices  9.83 us (32%)
  Pallas kernels  9.06 us (30%)
  between operations  0.68 us (2%)
    ppermute x10, starting transfers between devices, swap(): lax.ppermute(a, axis, [(i, i ^ mask) for i in range(lax.axis_size(axis))])  10.8 us
    ppermute x10, waiting for transfers between devices, swap(): lax.ppermute(a, axis, [(i, i ^ mask) for i in range(lax.axis_size(axis))])  9.83 us
    pallas_call x6, Pallas kernels, call(): pl.pallas_call(kernel, out_shape=[(pltpu.HBM if i < hbm_outs else pltpu.V...  9.06 us
  transfers between devices with their start and end apart: 10, of which 8 were waited for; matrix products, arithmetic and copies ran while one was open for 0% of the time, Pallas kernels for 17%

profile of v5, /device:TPU:0, one launch (start us, length us, event | category | flops | bytes accessed | tf_op | source)
XLA Modules:
  0.0 30.3 jit_solution(10474393781776847352)
XLA Ops:
  0.6 1.5 %states.1 = (f32[264,128]{1,0:T(8,128)S(1)}, f32[2,2,128,128]{3,2,1,0:T(8,128)S(1)}, f32[48,256]{1,0:T(8,128)S(1)}, bf16[768,256]{1,0:T(8,128)(2,1)S(1)}, bf16[768,256]{1,0:T(8,128)(2,1)S(1)}) custom-call(s32[2]{0:T(128)} %code_in.1, s32[6,128]{1,0:T(8,128)} %bitcast.1, bf16[768,256]{1,0:T(8,128)(2,1)} %k_in.1, bf16[768,256]{1,0:T(8,128)(2,1)} %v_in.1), custom_call_target="tpu_custom_call" | custom-call | flops 50331648 | bytes 2022408 | tf_op jit(solution)/shard_map/states/pallas_call | solution.py:350
  2.1 3.0 %collective-permute-start = (f32[264,128]{1,0:T(8,128)S(1)}, f32[264,128]{1,0:T(8,128)S(1)}, u32[]{:S(2)}, u32[]{:S(2)}) collective-permute-start(f32[264,128]{1,0:T(8,128)S(1)} %get-tuple-element.38.refs_0_), channel_id=1, source_target_pairs={{0,16},{8,24},{16,0},{24,8},{1,17},{9,25},{17,1},{25,9},{2,18},{10... | collective-permute-start | bytes 405512 | tf_op jit(solution)/shard_map/ppermute | solution.py:380
  5.2 0.0 collective-permute-start.1
  5.2 2.4 %within.1 = (bf16[3,2,256,256]{3,2,1,0:T(8,128)(2,1)S(1)}, f32[768,256]{1,0:T(8,128)S(1)}, f32[768,256]{1,0:T(8,128)S(1)}, f32[768,256]{1,0:T(8,128)S(1)}, bf16[...) custom-call(bf16[768,256]{1,0:T(8,128)(2,1)} %q_in.1, ...), custom_call_target="tpu_custom_call" | custom-call | flops 201326592 | bytes 5947392 | tf_op jit(solution)/shard_map/within/pallas_call | solution.py:350
  7.5 1.2 %collective-permute-done.refs_0_ = f32[264,128]{1,0:T(8,128)S(1)} collective-permute-done((f32[264,128]{1,0:T(8,128)S(1)}, f32[264,128]{1,0:T(8,128)S(1)}, u32[]{:S(2)}, u32[]{:S(2)}) %collective-permute-start) | collective-permute-done | bytes 135200 | tf_op jit(solution)/shard_map/ppermute | solution.py:380
  8.7 0.0 collective-permute-start.2
  8.7 0.0 collective-permute-done.1.refs_2_
  8.7 1.3 %collective-permute-done.2.refs_3_ = f32[264,128]{1,0:T(8,128)S(1)} collective-permute-done((f32[264,128]{1,0:T(8,128)S(1)}, f32[264,128]{1,0:T(8,128)S(1)}, u32[]{:S(2)}, u32[]{:S(2)}) %collective-permute-start.2) | collective-permute-done | bytes 135200 | tf_op jit(solution)/shard_map/ppermute | solution.py:380
  10.1 0.5 %attend.1 = (bf16[3,2,128,128]{3,2,1,0:T(8,128)(2,1)S(1)}, f32[768,256]{1,0:T(8,128)S(1)}, f32[8,256]{1,0:T(8,128)S(1)}) custom-call(f32[48,256]{1,0:T(8,128)S(1)} %get-tuple-element.29.factors_ref, bf16[768,256]{1,0:T(8,128)(2,1)S(1)} %get-tuple-element.32.q_ref, bf16[768,256]{1,0:T(8,128)(2,1)S(1)} %get-tuple-element.34.refs_1_.cot_ref, ...), custom_call_target="tpu_custom_call" | custom-call | flops 50331648 | bytes 4202496 | tf_op jit(solution)/shard_map/attend/pallas_call | solution.py:350
  10.6 2.8 %collective-permute-start.5 = (f32[8,256]{1,0:T(8,128)S(1)}, f32[8,256]{1,0:T(8,128)S(1)}, u32[]{:S(2)}, u32[]{:S(2)}) collective-permute-start(f32[8,256]{1,0:T(8,128)S(1)} %get-tuple-element.40), channel_id=1, source_target_pairs={{0,3},{1,2},{2,1},{3,0},{4,7},{5,6},{6,5},{7,4},{8,11},{9,10},{10,... | collective-permute-start | bytes 24584 | tf_op jit(solution)/shard_map/ppermute | solution.py:380
  13.4 0.4 %collective-permute-start.4 = (f32[8,256]{1,0:T(8,128)S(1)}, f32[8,256]{1,0:T(8,128)S(1)}, u32[]{:S(2)}, u32[]{:S(2)}) collective-permute-start(f32[8,256]{1,0:T(8,128)S(1)} %get-tuple-element.40), channel_id=1, source_target_pairs={{0,2},{1,3},{2,0},{3,1},{4,6},{5,7},{6,4},{7,5},{8,10},{9,11},{10,... | collective-permute-start | bytes 24584 | tf_op jit(solution)/shard_map/ppermute | solution.py:380
  13.9 0.3 %collective-permute-start.3 = (f32[8,256]{1,0:T(8,128)S(1)}, f32[8,256]{1,0:T(8,128)S(1)}, u32[]{:S(2)}, u32[]{:S(2)}) collective-permute-start(f32[8,256]{1,0:T(8,128)S(1)} %get-tuple-element.40), channel_id=1, source_target_pairs={{0,1},{1,0},{2,3},{3,2},{4,5},{5,4},{6,7},{7,6},{8,9},{9,8},{10,11... | collective-permute-start | bytes 24584 | tf_op jit(solution)/shard_map/ppermute | solution.py:380
  14.2 1.1 %collective-permute-done.5 = f32[8,256]{1,0:T(8,128)S(1)} collective-permute-done((f32[8,256]{1,0:T(8,128)S(1)}, f32[8,256]{1,0:T(8,128)S(1)}, u32[]{:S(2)}, u32[]{:S(2)}) %collective-permute-start.5) | collective-permute-done | bytes 8224 | tf_op jit(solution)/shard_map/ppermute | solution.py:380
  15.2 1.8 %collective-permute-done.4 = f32[8,256]{1,0:T(8,128)S(1)} collective-permute-done((f32[8,256]{1,0:T(8,128)S(1)}, f32[8,256]{1,0:T(8,128)S(1)}, u32[]{:S(2)}, u32[]{:S(2)}) %collective-permute-start.4) | collective-permute-done | bytes 8224 | tf_op jit(solution)/shard_map/ppermute | solution.py:380
  17.1 0.4 %collective-permute-done.3 = f32[8,256]{1,0:T(8,128)S(1)} collective-permute-done((f32[8,256]{1,0:T(8,128)S(1)}, f32[8,256]{1,0:T(8,128)S(1)}, u32[]{:S(2)}, u32[]{:S(2)}) %collective-permute-start.3) | collective-permute-done | bytes 8224 | tf_op jit(solution)/shard_map/ppermute | solution.py:380
  17.5 2.6 %collective-permute-start.6 = (f32[8,256]{1,0:T(8,128)S(1)}, f32[8,256]{1,0:T(8,128)S(1)}, u32[]{:S(2)}, u32[]{:S(2)}) collective-permute-start(f32[8,256]{1,0:T(8,128)S(1)} %add_add_fusion.refs_0_), channel_id=1, source_target_pairs={{0,4},{1,5},{2,6},{3,7},{4,0},{5,1},{6,2},{7,3},{8,12},{9,13},{10,... | collective-permute-start | bytes 24584 | tf_op jit(solution)/shard_map/ppermute | solution.py:380
  20.1 2.0 %collective-permute-done.6.refs_1_ = f32[8,256]{1,0:T(8,128)S(1)} collective-permute-done((f32[8,256]{1,0:T(8,128)S(1)}, f32[8,256]{1,0:T(8,128)S(1)}, u32[]{:S(2)}, u32[]{:S(2)}) %collective-permute-start.6) | collective-permute-done | bytes 8224 | tf_op jit(solution)/shard_map/ppermute | solution.py:380
  22.1 0.7 %grad.1 = (bf16[768,256]{1,0:T(8,128)(2,1)S(1)}, f32[8,256]{1,0:T(8,128)S(1)}, f32[264,128]{1,0:T(8,128)S(1)}, f32[2,2,128,128]{3,2,1,0:T(8,128)S(1)}) custom-call(f32[48,256]{1,0:T(8,128)S(1)} %get-tuple-element.29.factors_ref, bf16[3,2,128,256]{3,2,1,0:T(8,128)(2,1)S(1)} %get-tuple-element.33.lifted_ref, ...), custom_call_target="tpu_custom_call" | custom-call | flops 50331648 | bytes 2437120 | tf_op jit(solution)/shard_map/grad/pallas_call | solution.py:350
  22.7 1.6 %collective-permute-start.7 = (f32[264,128]{1,0:T(8,128)S(1)}, f32[264,128]{1,0:T(8,128)S(1)}, u32[]{:S(2)}, u32[]{:S(2)}) collective-permute-start(f32[264,128]{1,0:T(8,128)S(1)} %get-tuple-element.51.refs_0_), channel_id=1, source_target_pairs={{0,16},{8,24},{16,0},{24,8},{1,17},{9,25},{17,1},{25,9},{2,18},{10... | collective-permute-start | bytes 405512 | tf_op jit(solution)/shard_map/ppermute | solution.py:380
  24.3 0.0 collective-permute-start.8
  24.3 2.8 %inner_grads.1 = (bf16[768,256]{1,0:T(8,128)(2,1)}, bf16[768,256]{1,0:T(8,128)(2,1)}, f32[768,256]{1,0:T(8,128)S(1)}, f32[768,256]{1,0:T(8,128)S(1)}) custom-call(f32[48,256]{1,0:T(8,128)S(1)} %get-tuple-element.29.factors_ref, bf16[768,256]{1,0:T(8,128)(2,1)S(1)} %get-tuple-element.32.q_ref, bf16[768,256]{1,0:T(8,128)(2,1)S(1)} %get-tuple-element.30.k_ref, ...), custom_call_target="tpu_custom_call" | custom-call | flops 452984832 | bytes 6545408 | tf_op jit(solution)/shard_map/inner_grads/pallas_call | solution.py:350
  27.2 0.6 %collective-permute-done.7.refs_0_ = f32[264,128]{1,0:T(8,128)S(1)} collective-permute-done((f32[264,128]{1,0:T(8,128)S(1)}, f32[264,128]{1,0:T(8,128)S(1)}, u32[]{:S(2)}, u32[]{:S(2)}) %collective-permute-start.7) | collective-permute-done | bytes 135200 | tf_op jit(solution)/shard_map/ppermute | solution.py:380
  27.8 1.3 %collective-permute-done.9.refs_3_ = f32[264,128]{1,0:T(8,128)S(1)} collective-permute-done((f32[264,128]{1,0:T(8,128)S(1)}, f32[264,128]{1,0:T(8,128)S(1)}, u32[]{:S(2)}, u32[]{:S(2)}) %collective-permute-start.9) | collective-permute-done | bytes 135200 | tf_op jit(solution)/shard_map/ppermute | solution.py:380
  29.2 1.2 %outer_grads.1 = (bf16[768,256]{1,0:T(8,128)(2,1)}, bf16[768,256]{1,0:T(8,128)(2,1)}) custom-call(f32[48,256]{1,0:T(8,128)S(1)} %get-tuple-element.29.factors_ref, bf16[768,256]{1,0:T(8,128)(2,1)S(1)} %get-tuple-element.30.k_ref, bf16[768,256]{1,0:T(8,128)(2,1)S(1)} %get-tuple-element.31.v_ref, f32[768,256]{1,0:T(8,128)S(1)} %get-tuple-element.47.gk_part_ref, ...), custom_call_target="tpu_custom_call" | custom-call | flops 100663296 | bytes 4784128 | tf_op jit(solution)/shard_map/outer_grads/pallas_call | solution.py:350
  (5 shorter events, 0.0 us)
Async XLA Ops:
  2.1 6.6 %collective-permute-start = (f32[264,128]{1,0:T(8,128)S(1)}, f32[264,128]{1,0:T(8,128)S(1)}, u32[]{:S(2)}, u32[]{:S(2)}) collective-permute-start(f32[264,128]{1,0:T(8,128)S(1)} %get-tuple-element.38.refs_0_), channel_id=1, source_target_pairs={{0,16},{8,24},{16,0},{24,8},{1,17},{9,25},{17,1},{25,9},{2,18},{10... | collective-permute-start | bytes 405512 | tf_op jit(solution)/shard_map/ppermute | solution.py:380
  5.2 3.6 %collective-permute-start.1 = (f32[264,128]{1,0:T(8,128)S(1)}, f32[264,128]{1,0:T(8,128)S(1)}, u32[]{:S(2)}, u32[]{:S(2)}) collective-permute-start(f32[264,128]{1,0:T(8,128)S(1)} %get-tuple-element.38.refs_0_), channel_id=1, source_target_pairs={{0,8},{8,0},{16,24},{24,16},{1,9},{9,1},{17,25},{25,17},{2,10},{10... | collective-permute-start | bytes 405512 | tf_op jit(solution)/shard_map/ppermute | solution.py:380
  8.7 1.4 %collective-permute-start.2 = (f32[264,128]{1,0:T(8,128)S(1)}, f32[264,128]{1,0:T(8,128)S(1)}, u32[]{:S(2)}, u32[]{:S(2)}) collective-permute-start(f32[264,128]{1,0:T(8,128)S(1)} %after.2.refs_1_), channel_id=1, source_target_pairs={{0,8},{8,0},{16,24},{24,16},{1,9},{9,1},{17,25},{25,17},{2,10},{10... | collective-permute-start | bytes 405512 | tf_op jit(solution)/shard_map/ppermute | solution.py:380
  10.6 4.6 %collective-permute-start.5 = (f32[8,256]{1,0:T(8,128)S(1)}, f32[8,256]{1,0:T(8,128)S(1)}, u32[]{:S(2)}, u32[]{:S(2)}) collective-permute-start(f32[8,256]{1,0:T(8,128)S(1)} %get-tuple-element.40), channel_id=1, source_target_pairs={{0,3},{1,2},{2,1},{3,0},{4,7},{5,6},{6,5},{7,4},{8,11},{9,10},{10,... | collective-permute-start | bytes 24584 | tf_op jit(solution)/shard_map/ppermute | solution.py:380
  13.4 3.7 %collective-permute-start.4 = (f32[8,256]{1,0:T(8,128)S(1)}, f32[8,256]{1,0:T(8,128)S(1)}, u32[]{:S(2)}, u32[]{:S(2)}) collective-permute-start(f32[8,256]{1,0:T(8,128)S(1)} %get-tuple-element.40), channel_id=1, source_target_pairs={{0,2},{1,3},{2,0},{3,1},{4,6},{5,7},{6,4},{7,5},{8,10},{9,11},{10,... | collective-permute-start | bytes 24584 | tf_op jit(solution)/shard_map/ppermute | solution.py:380
  13.9 3.7 %collective-permute-start.3 = (f32[8,256]{1,0:T(8,128)S(1)}, f32[8,256]{1,0:T(8,128)S(1)}, u32[]{:S(2)}, u32[]{:S(2)}) collective-permute-start(f32[8,256]{1,0:T(8,128)S(1)} %get-tuple-element.40), channel_id=1, source_target_pairs={{0,1},{1,0},{2,3},{3,2},{4,5},{5,4},{6,7},{7,6},{8,9},{9,8},{10,11... | collective-permute-start | bytes 24584 | tf_op jit(solution)/shard_map/ppermute | solution.py:380
  17.5 4.5 %collective-permute-start.6 = (f32[8,256]{1,0:T(8,128)S(1)}, f32[8,256]{1,0:T(8,128)S(1)}, u32[]{:S(2)}, u32[]{:S(2)}) collective-permute-start(f32[8,256]{1,0:T(8,128)S(1)} %add_add_fusion.refs_0_), channel_id=1, source_target_pairs={{0,4},{1,5},{2,6},{3,7},{4,0},{5,1},{6,2},{7,3},{8,12},{9,13},{10,... | collective-permute-start | bytes 24584 | tf_op jit(solution)/shard_map/ppermute | solution.py:380
  22.7 5.1 %collective-permute-start.7 = (f32[264,128]{1,0:T(8,128)S(1)}, f32[264,128]{1,0:T(8,128)S(1)}, u32[]{:S(2)}, u32[]{:S(2)}) collective-permute-start(f32[264,128]{1,0:T(8,128)S(1)} %get-tuple-element.51.refs_0_), channel_id=1, source_target_pairs={{0,16},{8,24},{16,0},{24,8},{1,17},{9,25},{17,1},{25,9},{2,18},{10... | collective-permute-start | bytes 405512 | tf_op jit(solution)/shard_map/ppermute | solution.py:380
  24.3 3.5 %collective-permute-start.8 = (f32[264,128]{1,0:T(8,128)S(1)}, f32[264,128]{1,0:T(8,128)S(1)}, u32[]{:S(2)}, u32[]{:S(2)}) collective-permute-start(f32[264,128]{1,0:T(8,128)S(1)} %get-tuple-element.51.refs_0_), channel_id=1, source_target_pairs={{0,8},{8,0},{16,24},{24,16},{1,9},{9,1},{17,25},{25,17},{2,10},{10... | collective-permute-start | bytes 405512 | tf_op jit(solution)/shard_map/ppermute | solution.py:380
  27.8 1.4 %collective-permute-start.9 = (f32[264,128]{1,0:T(8,128)S(1)}, f32[264,128]{1,0:T(8,128)S(1)}, u32[]{:S(2)}, u32[]{:S(2)}) collective-permute-start(f32[264,128]{1,0:T(8,128)S(1)} %after.3.refs_1_), channel_id=1, source_target_pairs={{0,8},{8,0},{16,24},{24,16},{1,9},{9,1},{17,25},{25,17},{2,10},{10... | collective-permute-start | bytes 405512 | tf_op jit(solution)/shard_map/ppermute | solution.py:380

commit v6 on v5

--- a/solution.py
+++ b/solution.py
@@ -232,13 +232,16 @@
     squares, crosses = [], []
     for b in range(nb):
         rows = slice(b * BLK, (b + 1) * BLK)
-        carried = jnp.concatenate(
-            [mm(block(q_ref, b, h, e), held_ref[b, h]) for h in range(heads)], axis=1
-        )
-        att = within_ref[rows, :] + growth_ref[rows, :] * carried
-        att_ref[rows, :] = att
-        squares.append(row_sums(att * att))
-        crosses.append(row_sums(att * cot_ref[rows, :].astype(F32)))
+        square = cross = 0.0
+        for h in range(heads):
+            cols = slice(h * e, (h + 1) * e)
+            carried = mm(block(q_ref, b, h, e), held_ref[b, h])
+            att = within_ref[rows, cols] + growth_ref[rows, cols] * carried
+            att_ref[rows, cols] = att
+            square = square + att * att
+            cross = cross + att * cot_ref[rows, cols].astype(F32)
+        squares.append(row_sums(square))
+        crosses.append(row_sums(cross))
     parts = squares + crosses
     if up8(2 * nb) > 2 * nb:
         parts.append(jnp.zeros((up8(2 * nb) - 2 * nb, BLK), F32))

time: 30.5 us -> 30.5 us (level)
  no operation moved by 1% of the time
where the time goes in v6:
time: 30.5 us; the launch traced here: 30.3 us
  starting transfers between devices  10.8 us (35%)
  waiting for transfers between devices  9.83 us (32%)
  Pallas kernels  9.06 us (30%)
  between operations  0.68 us (2%)
    ppermute x10, starting transfers between devices, swap(): lax.ppermute(a, axis, [(i, i ^ mask) for i in range(lax.axis_size(axis))])  10.8 us
    ppermute x10, waiting for transfers between devices, swap(): lax.ppermute(a, axis, [(i, i ^ mask) for i in range(lax.axis_size(axis))])  9.83 us
    pallas_call x6, Pallas kernels, call(): pl.pallas_call(kernel, out_shape=[(pltpu.HBM if i < hbm_outs else pltpu.V...  9.06 us
  transfers between devices with their start and end apart: 10, of which 8 were waited for; matrix products, arithmetic and copies ran while one was open for 0% of the time, Pallas kernels for 17%

profile of v6, /device:TPU:0, one launch (start us, length us, event | category | flops | bytes accessed | tf_op | source)
XLA Modules:
  0.0 30.3 jit_solution(7501668955104292810)
XLA Ops:
  0.6 1.5 %states.1 = (f32[264,128]{1,0:T(8,128)S(1)}, f32[2,2,128,128]{3,2,1,0:T(8,128)S(1)}, f32[48,256]{1,0:T(8,128)S(1)}, bf16[768,256]{1,0:T(8,128)(2,1)S(1)}, bf16[768,256]{1,0:T(8,128)(2,1)S(1)}) custom-call(s32[2]{0:T(128)} %code_in.1, s32[6,128]{1,0:T(8,128)} %bitcast.1, bf16[768,256]{1,0:T(8,128)(2,1)} %k_in.1, bf16[768,256]{1,0:T(8,128)(2,1)} %v_in.1), custom_call_target="tpu_custom_call" | custom-call | flops 50331648 | bytes 2022408 | tf_op jit(solution)/shard_map/states/pallas_call | solution.py:353
  2.1 3.0 %collective-permute-start = (f32[264,128]{1,0:T(8,128)S(1)}, f32[264,128]{1,0:T(8,128)S(1)}, u32[]{:S(2)}, u32[]{:S(2)}) collective-permute-start(f32[264,128]{1,0:T(8,128)S(1)} %get-tuple-element.38.refs_0_), channel_id=1, source_target_pairs={{0,16},{8,24},{16,0},{24,8},{1,17},{9,25},{17,1},{25,9},{2,18},{10... | collective-permute-start | bytes 405512 | tf_op jit(solution)/shard_map/ppermute | solution.py:383
  5.2 2.4 %within.1 = (bf16[3,2,256,256]{3,2,1,0:T(8,128)(2,1)S(1)}, f32[768,256]{1,0:T(8,128)S(1)}, f32[768,256]{1,0:T(8,128)S(1)}, f32[768,256]{1,0:T(8,128)S(1)}, bf16[...) custom-call(bf16[768,256]{1,0:T(8,128)(2,1)} %q_in.1, ...), custom_call_target="tpu_custom_call" | custom-call | flops 201326592 | bytes 5947392 | tf_op jit(solution)/shard_map/within/pallas_call | solution.py:353
  7.5 1.2 %collective-permute-done.refs_0_ = f32[264,128]{1,0:T(8,128)S(1)} collective-permute-done((f32[264,128]{1,0:T(8,128)S(1)}, f32[264,128]{1,0:T(8,128)S(1)}, u32[]{:S(2)}, u32[]{:S(2)}) %collective-permute-start) | collective-permute-done | bytes 135200 | tf_op jit(solution)/shard_map/ppermute | solution.py:383
  8.7 0.0 collective-permute-start.2
  8.7 0.0 collective-permute-done.1.refs_2_
  8.7 1.3 %collective-permute-done.2.refs_3_ = f32[264,128]{1,0:T(8,128)S(1)} collective-permute-done((f32[264,128]{1,0:T(8,128)S(1)}, f32[264,128]{1,0:T(8,128)S(1)}, u32[]{:S(2)}, u32[]{:S(2)}) %collective-permute-start.2) | collective-permute-done | bytes 135200 | tf_op jit(solution)/shard_map/ppermute | solution.py:383
  10.1 0.5 %attend.1 = (bf16[3,2,128,128]{3,2,1,0:T(8,128)(2,1)S(1)}, f32[768,256]{1,0:T(8,128)S(1)}, f32[8,256]{1,0:T(8,128)S(1)}) custom-call(f32[48,256]{1,0:T(8,128)S(1)} %get-tuple-element.29.factors_ref, bf16[768,256]{1,0:T(8,128)(2,1)S(1)} %get-tuple-element.32.q_ref, bf16[768,256]{1,0:T(8,128)(2,1)S(1)} %get-tuple-element.34.refs_1_.cot_ref, ...), custom_call_target="tpu_custom_call" | custom-call | flops 50331648 | bytes 4202496 | tf_op jit(solution)/shard_map/attend/pallas_call | solution.py:353
  10.6 2.8 %collective-permute-start.5 = (f32[8,256]{1,0:T(8,128)S(1)}, f32[8,256]{1,0:T(8,128)S(1)}, u32[]{:S(2)}, u32[]{:S(2)}) collective-permute-start(f32[8,256]{1,0:T(8,128)S(1)} %get-tuple-element.40), channel_id=1, source_target_pairs={{0,3},{1,2},{2,1},{3,0},{4,7},{5,6},{6,5},{7,4},{8,11},{9,10},{10,... | collective-permute-start | bytes 24584 | tf_op jit(solution)/shard_map/ppermute | solution.py:383
  13.4 0.4 %collective-permute-start.4 = (f32[8,256]{1,0:T(8,128)S(1)}, f32[8,256]{1,0:T(8,128)S(1)}, u32[]{:S(2)}, u32[]{:S(2)}) collective-permute-start(f32[8,256]{1,0:T(8,128)S(1)} %get-tuple-element.40), channel_id=1, source_target_pairs={{0,2},{1,3},{2,0},{3,1},{4,6},{5,7},{6,4},{7,5},{8,10},{9,11},{10,... | collective-permute-start | bytes 24584 | tf_op jit(solution)/shard_map/ppermute | solution.py:383
  13.9 0.3 %collective-permute-start.3 = (f32[8,256]{1,0:T(8,128)S(1)}, f32[8,256]{1,0:T(8,128)S(1)}, u32[]{:S(2)}, u32[]{:S(2)}) collective-permute-start(f32[8,256]{1,0:T(8,128)S(1)} %get-tuple-element.40), channel_id=1, source_target_pairs={{0,1},{1,0},{2,3},{3,2},{4,5},{5,4},{6,7},{7,6},{8,9},{9,8},{10,11... | collective-permute-start | bytes 24584 | tf_op jit(solution)/shard_map/ppermute | solution.py:383
  14.2 1.1 %collective-permute-done.5 = f32[8,256]{1,0:T(8,128)S(1)} collective-permute-done((f32[8,256]{1,0:T(8,128)S(1)}, f32[8,256]{1,0:T(8,128)S(1)}, u32[]{:S(2)}, u32[]{:S(2)}) %collective-permute-start.5) | collective-permute-done | bytes 8224 | tf_op jit(solution)/shard_map/ppermute | solution.py:383
  15.2 1.8 %collective-permute-done.4 = f32[8,256]{1,0:T(8,128)S(1)} collective-permute-done((f32[8,256]{1,0:T(8,128)S(1)}, f32[8,256]{1,0:T(8,128)S(1)}, u32[]{:S(2)}, u32[]{:S(2)}) %collective-permute-start.4) | collective-permute-done | bytes 8224 | tf_op jit(solution)/shard_map/ppermute | solution.py:383
  17.1 0.4 %collective-permute-done.3 = f32[8,256]{1,0:T(8,128)S(1)} collective-permute-done((f32[8,256]{1,0:T(8,128)S(1)}, f32[8,256]{1,0:T(8,128)S(1)}, u32[]{:S(2)}, u32[]{:S(2)}) %collective-permute-start.3) | collective-permute-done | bytes 8224 | tf_op jit(solution)/shard_map/ppermute | solution.py:383
  17.5 2.6 %collective-permute-start.6 = (f32[8,256]{1,0:T(8,128)S(1)}, f32[8,256]{1,0:T(8,128)S(1)}, u32[]{:S(2)}, u32[]{:S(2)}) collective-permute-start(f32[8,256]{1,0:T(8,128)S(1)} %add_add_fusion.refs_0_), channel_id=1, source_target_pairs={{0,4},{1,5},{2,6},{3,7},{4,0},{5,1},{6,2},{7,3},{8,12},{9,13},{10,... | collective-permute-start | bytes 24584 | tf_op jit(solution)/shard_map/ppermute | solution.py:383
  20.1 2.0 %collective-permute-done.6.refs_1_ = f32[8,256]{1,0:T(8,128)S(1)} collective-permute-done((f32[8,256]{1,0:T(8,128)S(1)}, f32[8,256]{1,0:T(8,128)S(1)}, u32[]{:S(2)}, u32[]{:S(2)}) %collective-permute-start.6) | collective-permute-done | bytes 8224 | tf_op jit(solution)/shard_map/ppermute | solution.py:383
  22.1 0.7 %grad.1 = (bf16[768,256]{1,0:T(8,128)(2,1)S(1)}, f32[8,256]{1,0:T(8,128)S(1)}, f32[264,128]{1,0:T(8,128)S(1)}, f32[2,2,128,128]{3,2,1,0:T(8,128)S(1)}) custom-call(f32[48,256]{1,0:T(8,128)S(1)} %get-tuple-element.29.factors_ref, bf16[3,2,128,256]{3,2,1,0:T(8,128)(2,1)S(1)} %get-tuple-element.33.lifted_ref, ...), custom_call_target="tpu_custom_call" | custom-call | flops 50331648 | bytes 2437120 | tf_op jit(solution)/shard_map/grad/pallas_call | solution.py:353
  22.8 1.6 %collective-permute-start.7 = (f32[264,128]{1,0:T(8,128)S(1)}, f32[264,128]{1,0:T(8,128)S(1)}, u32[]{:S(2)}, u32[]{:S(2)}) collective-permute-start(f32[264,128]{1,0:T(8,128)S(1)} %get-tuple-element.51.refs_0_), channel_id=1, source_target_pairs={{0,16},{8,24},{16,0},{24,8},{1,17},{9,25},{17,1},{25,9},{2,18},{10... | collective-permute-start | bytes 405512 | tf_op jit(solution)/shard_map/ppermute | solution.py:383
  24.3 2.8 %inner_grads.1 = (bf16[768,256]{1,0:T(8,128)(2,1)}, bf16[768,256]{1,0:T(8,128)(2,1)}, f32[768,256]{1,0:T(8,128)S(1)}, f32[768,256]{1,0:T(8,128)S(1)}) custom-call(f32[48,256]{1,0:T(8,128)S(1)} %get-tuple-element.29.factors_ref, bf16[768,256]{1,0:T(8,128)(2,1)S(1)} %get-tuple-element.32.q_ref, bf16[768,256]{1,0:T(8,128)(2,1)S(1)} %get-tuple-element.30.k_ref, ...), custom_call_target="tpu_custom_call" | custom-call | flops 452984832 | bytes 6545408 | tf_op jit(solution)/shard_map/inner_grads/pallas_call | solution.py:353
  27.2 0.6 %collective-permute-done.7.refs_0_ = f32[264,128]{1,0:T(8,128)S(1)} collective-permute-done((f32[264,128]{1,0:T(8,128)S(1)}, f32[264,128]{1,0:T(8,128)S(1)}, u32[]{:S(2)}, u32[]{:S(2)}) %collective-permute-start.7) | collective-permute-done | bytes 135200 | tf_op jit(solution)/shard_map/ppermute | solution.py:383
  27.8 0.0 collective-permute-start.9
  27.8 0.0 collective-permute-done.8.refs_2_
  27.8 1.3 %collective-permute-done.9.refs_3_ = f32[264,128]{1,0:T(8,128)S(1)} collective-permute-done((f32[264,128]{1,0:T(8,128)S(1)}, f32[264,128]{1,0:T(8,128)S(1)}, u32[]{:S(2)}, u32[]{:S(2)}) %collective-permute-start.9) | collective-permute-done | bytes 135200 | tf_op jit(solution)/shard_map/ppermute | solution.py:383
  29.2 1.2 %outer_grads.1 = (bf16[768,256]{1,0:T(8,128)(2,1)}, bf16[768,256]{1,0:T(8,128)(2,1)}) custom-call(f32[48,256]{1,0:T(8,128)S(1)} %get-tuple-element.29.factors_ref, bf16[768,256]{1,0:T(8,128)(2,1)S(1)} %get-tuple-element.30.k_ref, bf16[768,256]{1,0:T(8,128)(2,1)S(1)} %get-tuple-element.31.v_ref, f32[768,256]{1,0:T(8,128)S(1)} %get-tuple-element.47.gk_part_ref, ...), custom_call_target="tpu_custom_call" | custom-call | flops 100663296 | bytes 4784128 | tf_op jit(solution)/shard_map/outer_grads/pallas_call | solution.py:353
  (5 shorter events, 0.0 us)
Async XLA Ops:
  2.1 6.6 %collective-permute-start = (f32[264,128]{1,0:T(8,128)S(1)}, f32[264,128]{1,0:T(8,128)S(1)}, u32[]{:S(2)}, u32[]{:S(2)}) collective-permute-start(f32[264,128]{1,0:T(8,128)S(1)} %get-tuple-element.38.refs_0_), channel_id=1, source_target_pairs={{0,16},{8,24},{16,0},{24,8},{1,17},{9,25},{17,1},{25,9},{2,18},{10... | collective-permute-start | bytes 405512 | tf_op jit(solution)/shard_map/ppermute | solution.py:383
  5.2 3.6 %collective-permute-start.1 = (f32[264,128]{1,0:T(8,128)S(1)}, f32[264,128]{1,0:T(8,128)S(1)}, u32[]{:S(2)}, u32[]{:S(2)}) collective-permute-start(f32[264,128]{1,0:T(8,128)S(1)} %get-tuple-element.38.refs_0_), channel_id=1, source_target_pairs={{0,8},{8,0},{16,24},{24,16},{1,9},{9,1},{17,25},{25,17},{2,10},{10... | collective-permute-start | bytes 405512 | tf_op jit(solution)/shard_map/ppermute | solution.py:383
  8.7 1.4 %collective-permute-start.2 = (f32[264,128]{1,0:T(8,128)S(1)}, f32[264,128]{1,0:T(8,128)S(1)}, u32[]{:S(2)}, u32[]{:S(2)}) collective-permute-start(f32[264,128]{1,0:T(8,128)S(1)} %after.2.refs_1_), channel_id=1, source_target_pairs={{0,8},{8,0},{16,24},{24,16},{1,9},{9,1},{17,25},{25,17},{2,10},{10... | collective-permute-start | bytes 405512 | tf_op jit(solution)/shard_map/ppermute | solution.py:383
  10.6 4.6 %collective-permute-start.5 = (f32[8,256]{1,0:T(8,128)S(1)}, f32[8,256]{1,0:T(8,128)S(1)}, u32[]{:S(2)}, u32[]{:S(2)}) collective-permute-start(f32[8,256]{1,0:T(8,128)S(1)} %get-tuple-element.40), channel_id=1, source_target_pairs={{0,3},{1,2},{2,1},{3,0},{4,7},{5,6},{6,5},{7,4},{8,11},{9,10},{10,... | collective-permute-start | bytes 24584 | tf_op jit(solution)/shard_map/ppermute | solution.py:383
  13.4 3.7 %collective-permute-start.4 = (f32[8,256]{1,0:T(8,128)S(1)}, f32[8,256]{1,0:T(8,128)S(1)}, u32[]{:S(2)}, u32[]{:S(2)}) collective-permute-start(f32[8,256]{1,0:T(8,128)S(1)} %get-tuple-element.40), channel_id=1, source_target_pairs={{0,2},{1,3},{2,0},{3,1},{4,6},{5,7},{6,4},{7,5},{8,10},{9,11},{10,... | collective-permute-start | bytes 24584 | tf_op jit(solution)/shard_map/ppermute | solution.py:383
  13.9 3.7 %collective-permute-start.3 = (f32[8,256]{1,0:T(8,128)S(1)}, f32[8,256]{1,0:T(8,128)S(1)}, u32[]{:S(2)}, u32[]{:S(2)}) collective-permute-start(f32[8,256]{1,0:T(8,128)S(1)} %get-tuple-element.40), channel_id=1, source_target_pairs={{0,1},{1,0},{2,3},{3,2},{4,5},{5,4},{6,7},{7,6},{8,9},{9,8},{10,11... | collective-permute-start | bytes 24584 | tf_op jit(solution)/shard_map/ppermute | solution.py:383
  17.5 4.5 %collective-permute-start.6 = (f32[8,256]{1,0:T(8,128)S(1)}, f32[8,256]{1,0:T(8,128)S(1)}, u32[]{:S(2)}, u32[]{:S(2)}) collective-permute-start(f32[8,256]{1,0:T(8,128)S(1)} %add_add_fusion.refs_0_), channel_id=1, source_target_pairs={{0,4},{1,5},{2,6},{3,7},{4,0},{5,1},{6,2},{7,3},{8,12},{9,13},{10,... | collective-permute-start | bytes 24584 | tf_op jit(solution)/shard_map/ppermute | solution.py:383
  22.8 5.1 %collective-permute-start.7 = (f32[264,128]{1,0:T(8,128)S(1)}, f32[264,128]{1,0:T(8,128)S(1)}, u32[]{:S(2)}, u32[]{:S(2)}) collective-permute-start(f32[264,128]{1,0:T(8,128)S(1)} %get-tuple-element.51.refs_0_), channel_id=1, source_target_pairs={{0,16},{8,24},{16,0},{24,8},{1,17},{9,25},{17,1},{25,9},{2,18},{10... | collective-permute-start | bytes 405512 | tf_op jit(solution)/shard_map/ppermute | solution.py:383
  24.3 3.5 %collective-permute-start.8 = (f32[264,128]{1,0:T(8,128)S(1)}, f32[264,128]{1,0:T(8,128)S(1)}, u32[]{:S(2)}, u32[]{:S(2)}) collective-permute-start(f32[264,128]{1,0:T(8,128)S(1)} %get-tuple-element.51.refs_0_), channel_id=1, source_target_pairs={{0,8},{8,0},{16,24},{24,16},{1,9},{9,1},{17,25},{25,17},{2,10},{10... | collective-permute-start | bytes 405512 | tf_op jit(solution)/shard_map/ppermute | solution.py:383
  27.8 1.4 %collective-permute-start.9 = (f32[264,128]{1,0:T(8,128)S(1)}, f32[264,128]{1,0:T(8,128)S(1)}, u32[]{:S(2)}, u32[]{:S(2)}) collective-permute-start(f32[264,128]{1,0:T(8,128)S(1)} %after.3.refs_1_), channel_id=1, source_target_pairs={{0,8},{8,0},{16,24},{24,16},{1,9},{9,1},{17,25},{25,17},{2,10},{10... | collective-permute-start | bytes 405512 | tf_op jit(solution)/shard_map/ppermute | solution.py:383
